TPU v7x, 32 devices: a whole 2x2x4 slice. The times are simulated.
32 devices in a mesh: row: 8 (over y, x, core), col: 4 (over z).
Axes of the slice: x: 2, y: 2, z: 4, core: 2. Of those that a mesh axis runs over, the one named last changes fastest.
Arguments:
- before_scan: float32 [4, 2048, 4096], P(None, 'row', 'col'), may hold values from -40 to 40
- after_scan: float32 [4, 2048, 4096], P(None, 'row', 'col'), may hold values from -40 to 40
- drift_offsets: int32 [2, 4, 8, 4], P(None, None, 'row', 'col'), may hold values from -128 to 128, as said below
- drift_fractions: int32 [2, 4, 8, 4], P(None, None, 'row', 'col'), may hold values from 0 to 255
Outputs:
- band_field: float32 [4, 2048, 4096], P(None, 'row', 'col')
- slope_field: float32 [4, 2048, 4096], P(None, 'row', 'col')
- surface_params: float32 [2, 4], replicated
Inputs may be any that keep to these rules, and one draw needn't show every extreme that they name: `drift_offsets`: for every scan and tile, the cells a tile reads (its own cells shifted by its offsets, widened by one row and column before and two after) lie inside the window. In every scan the first tile has offsets 128, 128 and the last tile minus 128, minus 128.
All inputs are finite; a program needn't handle non-finite values.
Results may differ from a plain program's by a relative error of at most 0.00014.
Values sent between devices are 32-bit elements; how exact they have to be, the bound alone decides.
A program may use at most 128 MiB of HBM per device.

v0:
```python
import math

import jax
import jax.numpy as jnp
from jax import lax
from jax.sharding import PartitionSpec as P

LS = 5
SR = 4
LCUT = 1600
BLOCK = 16
DRIFT = 128


ALPHA = math.sqrt(math.log(2.0) / math.pi)
SPACING = 0.5
EPSILON = 1e-06
HIGHEST = lax.Precision.HIGHEST


def with_halo(value, sides, width):
    for axis, dim in sides:
        count, length = (lax.axis_size(axis), value.shape[dim])
        up = [(i, (i + 1) % count) for i in range(count - 1)]
        down = [(j, i) for i, j in up]
        last = lax.slice_in_dim(value, length - width, length, axis=dim)
        leading = lax.slice_in_dim(value, 0, width, axis=dim)
        before = lax.ppermute(last, axis, up)
        after = lax.ppermute(leading, axis, down)
        value = jnp.concatenate([before, value, after], axis=dim)
    return value


def cubic_weights(fraction):
    position = fraction.astype(jnp.float32) / 256.0
    square = position * position
    cube_term = square * position
    return (
        0.5 * (2.0 * square - cube_term - position),
        0.5 * (3.0 * cube_term - 5.0 * square + 2.0),
        0.5 * (4.0 * square - 3.0 * cube_term + position),
        0.5 * (cube_term - square),
    )


def interpolate(window, row_taps, col_taps):
    height = window.shape[0] - 3
    length = window.shape[1] - 3
    across = (
        row_taps[0] * window[0:height]
        + row_taps[1] * window[1 : height + 1]
        + row_taps[2] * window[2 : height + 2]
        + row_taps[3] * window[3 : height + 3]
    )
    return (
        col_taps[0] * across[:, 0:length]
        + col_taps[1] * across[:, 1 : length + 1]
        + col_taps[2] * across[:, 2 : length + 2]
        + col_taps[3] * across[:, 3 : length + 3]
    )


def resample(after_scan, drift_offsets, drift_fractions):
    height, length = (after_scan.shape[1], after_scan.shape[2])
    margin = DRIFT + 2
    widened = with_halo(after_scan, (("row", 1), ("col", 2)), margin)
    row_taps = jnp.stack(cubic_weights(drift_fractions[0, :, 0, 0]), axis=-1)
    col_taps = jnp.stack(cubic_weights(drift_fractions[1, :, 0, 0]), axis=-1)

    def one_scan(window, row_shift, col_shift, row_weights, col_weights):
        source = lax.dynamic_slice(
            window, (margin - 1 + row_shift, margin - 1 + col_shift), (height + 3, length + 3)
        )
        return interpolate(source, row_weights, col_weights)

    return jax.vmap(one_scan)(
        widened, drift_offsets[0, :, 0, 0], drift_offsets[1, :, 0, 0], row_taps, col_taps
    )


def short_taps():
    return [math.exp(-math.pi * (offset / (ALPHA * LS)) ** 2) for offset in range(-SR, SR + 1)]


def short_filter(widened, height, length):
    kernel_taps = short_taps()
    column_index = (
        lax.axis_index("col") * length - SR + jnp.arange(length + 2 * SR, dtype=jnp.int32)
    )
    column_inside = ((column_index >= 0) & (column_index < length * lax.axis_size("col"))).astype(
        jnp.float32
    )
    summed = kernel_taps[0] * widened[:, :, 0:length]
    weight = kernel_taps[0] * column_inside[0:length]
    for offset in range(1, 2 * SR + 1):
        summed = summed + kernel_taps[offset] * widened[:, :, offset : offset + length]
        weight = weight + kernel_taps[offset] * column_inside[offset : offset + length]
    across = summed / weight
    row_index = lax.axis_index("row") * height - SR + jnp.arange(height + 2 * SR, dtype=jnp.int32)
    row_inside = ((row_index >= 0) & (row_index < height * lax.axis_size("row"))).astype(
        jnp.float32
    )
    summed = kernel_taps[0] * across[:, 0:height, :]
    weight = kernel_taps[0] * row_inside[0:height]
    for offset in range(1, 2 * SR + 1):
        summed = summed + kernel_taps[offset] * across[:, offset : offset + height, :]
        weight = weight + kernel_taps[offset] * row_inside[offset : offset + height]
    return summed / weight[:, None]


def coarse_means(surface):
    scans, height, length = surface.shape
    return surface.reshape(scans, height // BLOCK, BLOCK, length // BLOCK, BLOCK).mean(axis=(2, 4))


def gauss_block(source, target):
    distance = ((source[:, None] - target[None, :]) * BLOCK).astype(jnp.float32) / (ALPHA * LCUT)
    return jnp.exp(-math.pi * distance * distance)


def long_cols(coarse):
    width = coarse.shape[2]
    target = lax.axis_index("col") * width + jnp.arange(width, dtype=jnp.int32)
    portion = lax.all_gather(coarse, "col", axis=2, tiled=True)
    source = jnp.arange(portion.shape[2], dtype=jnp.int32)
    matrix = gauss_block(source, target)
    summed = jnp.einsum("frk,kc->frc", portion, matrix, precision=HIGHEST)
    weight = jnp.sum(matrix, axis=0)
    return summed / weight


def long_rows(surface):
    rows_here = surface.shape[1]
    target = lax.axis_index("row") * rows_here + jnp.arange(rows_here, dtype=jnp.int32)
    portion = lax.all_gather(surface, "row", axis=1, tiled=True)
    source = jnp.arange(portion.shape[1], dtype=jnp.int32)
    matrix = gauss_block(target, source)
    summed = jnp.einsum("rk,fkc->frc", matrix, portion, precision=HIGHEST)
    weight = jnp.sum(matrix, axis=1)
    return summed / weight[:, None]


def upsample_matrix(fine_index, coarse_index, coarse_count):
    numerator = 2 * fine_index + 1 - BLOCK
    lower_index = numerator // (2 * BLOCK)
    fraction = (numerator - lower_index * (2 * BLOCK)).astype(jnp.float32) / (2.0 * BLOCK)
    outside = (lower_index < 0) | (lower_index >= coarse_count - 1)
    fraction = jnp.where(outside, jnp.zeros_like(fraction), fraction)
    lower_index = jnp.clip(lower_index, 0, coarse_count - 1)
    first_part = (coarse_index[None, :] == lower_index[:, None]).astype(jnp.float32) * (
        1.0 - fraction
    )[:, None]
    second_part = (coarse_index[None, :] == (lower_index + 1)[:, None]).astype(
        jnp.float32
    ) * fraction[:, None]
    return first_part + second_part


def upsample(wavy_coarse, height, length):
    coarse_rows, coarse_cols = (wavy_coarse.shape[1], wavy_coarse.shape[2])
    widened_coarse = with_halo(wavy_coarse, (("row", 1), ("col", 2)), 1)
    row_fine = lax.axis_index("row") * height + jnp.arange(height, dtype=jnp.int32)
    row_blocks = (
        lax.axis_index("row") * coarse_rows - 1 + jnp.arange(coarse_rows + 2, dtype=jnp.int32)
    )
    col_fine = lax.axis_index("col") * length + jnp.arange(length, dtype=jnp.int32)
    col_blocks = (
        lax.axis_index("col") * coarse_cols - 1 + jnp.arange(coarse_cols + 2, dtype=jnp.int32)
    )
    row_up = upsample_matrix(row_fine, row_blocks, coarse_rows * lax.axis_size("row"))
    col_up = upsample_matrix(col_fine, col_blocks, coarse_cols * lax.axis_size("col"))
    row_mixed = jnp.einsum("pa,sab->spb", row_up, widened_coarse, precision=HIGHEST)
    return jnp.einsum("spb,qb->spq", row_mixed, col_up, precision=HIGHEST)


def slopes(surface):
    height, length = (surface.shape[1], surface.shape[2])
    bordered = with_halo(surface, (("row", 1), ("col", 2)), 1)
    column_index = lax.axis_index("col") * length + jnp.arange(length, dtype=jnp.int32)
    row_index = lax.axis_index("row") * height + jnp.arange(height, dtype=jnp.int32)
    column_mask = (
        (column_index >= 1) & (column_index <= length * lax.axis_size("col") - 2)
    ).astype(jnp.float32)
    row_mask = ((row_index >= 1) & (row_index <= height * lax.axis_size("row") - 2)).astype(
        jnp.float32
    )
    along_cols = (bordered[:, 1:-1, 2:] - bordered[:, 1:-1, :-2]) / (2.0 * SPACING) * column_mask
    along_rows = (
        (bordered[:, 2:, 1:-1] - bordered[:, :-2, 1:-1]) / (2.0 * SPACING) * row_mask[:, None]
    )
    return along_cols * along_cols + along_rows * along_rows


def body(before_scan, after_scan, drift_offsets, drift_fractions):
    height, length = (before_scan.shape[1], before_scan.shape[2])
    shifted = resample(after_scan, drift_offsets, drift_fractions)
    difference = before_scan - shifted
    widened = with_halo(difference, (("row", 1), ("col", 2)), SR)
    smooth = short_filter(widened, height, length)
    coarse = coarse_means(smooth)
    wavy_coarse = long_rows(long_cols(coarse))
    waviness = upsample(wavy_coarse, height, length)
    band_field = smooth - waviness
    slope_field = slopes(band_field)
    height_sq = jnp.sum(band_field * band_field, axis=(1, 2))
    slope_sum = jnp.sum(slope_field, axis=(1, 2))
    height_all, slope_all = lax.psum((height_sq, slope_sum), ("row", "col"))
    total_cells = height * lax.axis_size("row") * length * lax.axis_size("col")
    surface_params = jnp.sqrt(jnp.stack([height_all, slope_all]) / total_cells + EPSILON)
    return (band_field, slope_field, surface_params)


def solution(mesh):
    in_specs = (
        P(None, "row", "col"),
        P(None, "row", "col"),
        P(None, None, "row", "col"),
        P(None, None, "row", "col"),
    )
    out_specs = (P(None, "row", "col"), P(None, "row", "col"), P())
    return jax.shard_map(body, mesh=mesh, in_specs=in_specs, out_specs=out_specs, check_vma=False)
```

profile of v0, /device:TPU:0, one launch (start us, length us, event | category | flops | bytes accessed | tf_op | source)
XLA Modules:
  0.0 378.3 jit_solution(1989362204232394107)
XLA Ops:
  0.6 3.2 fusion.118
  3.9 1.4 copy.42
  5.3 3.8 collective-permute-start
  9.0 2.7 copy.43
  11.7 1.4 collective-permute-start.1
  13.1 5.2 %copy.28 = f32[4,256,1024]{1,0,2:T(4,128)} copy(f32[4,256,1024]{2,1,0:T(8,128)} %param.5) | data formatting | bytes 8388608 | tf_op args[1]
  18.6 6.3 %copy.27 = f32[4,130,1024]{1,0,2:T(4,128)} copy(f32[4,130,1024]{2,0,1:T(4,128)} %collective-permute-done) | data formatting | bytes 4259840 | tf_op jit(solution)/shard_map/ppermute | solution.py:28
  24.8 6.2 %copy.29 = f32[4,130,1024]{1,0,2:T(4,128)} copy(f32[4,130,1024]{2,0,1:T(4,128)} %collective-permute-done.1) | data formatting | bytes 4259840 | tf_op jit(solution)/shard_map/ppermute | solution.py:29
  31.0 3.5 pad_maximum_fusion.13
  34.5 4.4 %collective-permute-start.2 = (f32[4,516,130]{1,0,2:T(4,128)S(1)}, f32[4,516,130]{1,0,2:T(4,128)S(1)}, u32[]{:S(2)}, u32[]{:S(2)}) collective-permute-start(f32[4,516,130]{1,0,2:T(4,128)S(1)} %get-tuple-element.42), channel_id=1, source_target_pairs={{0,1},{1,2},{2,3},{4,5},{5,6},{6,7},{8,9},{9,10},{10,11},{12,13},{... | collective-permute-start | bytes 3219848 | tf_op jit(solution)/shard_map/ppermute | solution.py:28
  38.9 1.5 collective-permute-start.3
  41.0 13.2 %collective-permute-done.2 = f32[4,516,130]{1,0,2:T(4,128)S(1)} collective-permute-done((f32[4,516,130]{1,0,2:T(4,128)S(1)}, f32[4,516,130]{1,0,2:T(4,128)S(1)}, u32[]{:S(2)}, u32[]{:S(2)}) %collective-permute-start.2) | collective-permute-done | bytes 1073312 | tf_op jit(solution)/shard_map/ppermute | solution.py:28
  54.2 4.5 %collective-permute-done.3 = f32[4,516,130]{1,0,2:T(4,128)S(1)} collective-permute-done((f32[4,516,130]{1,0,2:T(4,128)S(1)}, f32[4,516,130]{1,0,2:T(4,128)S(1)}, u32[]{:S(2)}, u32[]{:S(2)}) %collective-permute-start.3) | collective-permute-done | bytes 1073312 | tf_op jit(solution)/shard_map/ppermute | solution.py:29
  58.6 29.5 %pad_maximum_fusion = f32[4,516,1284]{1,0,2:T(4,128)} fusion(f32[4,516,130]{1,0,2:T(4,128)S(1)} %collective-permute-done.3, f32[4,130,1024]{1,0,2:T(4,128)} %copy.29, f32[4,256,1024]{1,0,2:T(4,128)S(1)} %copy-done.2, f32[4,130,1024]{1,0,2:T(4,128)} %copy.27, f32[4,516,130]{1,0,2:T(4,128)S(1)} %collective-permute-done.2), kind=kLoop, calls=%fused_computation.2 | loop fusion | flops 10600704 | bytes 21201408 | tf_op jit(solution)/shard_map/concatenate | solution.py:30
  88.1 15.3 %copy.30 = f32[4,516,1284]{2,1,0:T(8,128)} copy(f32[4,516,1284]{1,0,2:T(4,128)} %pad_maximum_fusion) | data formatting | bytes 21201408
  103.4 21.3 %while.1 = (s32[]{:T(128)}, f32[4,516,1284]{2,1,0:T(8,128)}, s32[4,3]{1,0:T(4,128)S(1)}, f32[4,259,1027]{2,1,0:T(8,128)}, s32[]{:T(128)}) while((s32[]{:T(128)}, f32[4,516,1284]{2,1,0:T(8,128)}, s32[4,3]{1,0:T(4,128)S(1)}, f32[4,259,1027]{2,1,0:T(8,128)}, s32[]{:T(128)}) %tuple.51), condition=%wide.while_cond, body=%wide.while_body.sunk | while | flops 2 | bytes 2435185 | solution.py:71
  104.0 4.7 %dynamic-slice_dynamic-update-slice_fusion.2 = f32[4,259,1027]{2,1,0:T(8,128)} fusion(f32[4,259,1027]{2,1,0:T(8,128)} %get-tuple-element.118, s32[]{:T(128)} %get-tuple-element.115, f32[4,516,1284]{2,1,0:T(8,128)} %get-tuple-element.121, s32[]{:T(128)} %bitcast.84, s32[]{:T(128)} %bitcast.85, s32[]{:T(128)} %bitcast.86), kind=kLoop, calls=%fused_computation.clone.1 | loop fusion | bytes 2435072 | tf_op jit(solution)/shard_map/vmap()/gather
  109.4 4.6 %dynamic-slice_dynamic-update-slice_fusion.2 = f32[4,259,1027]{2,1,0:T(8,128)} fusion(f32[4,259,1027]{2,1,0:T(8,128)} %get-tuple-element.118, s32[]{:T(128)} %get-tuple-element.115, f32[4,516,1284]{2,1,0:T(8,128)} %get-tuple-element.121, s32[]{:T(128)} %bitcast.84, s32[]{:T(128)} %bitcast.85, s32[]{:T(128)} %bitcast.86), kind=kLoop, calls=%fused_computation.clone.1 | loop fusion | bytes 2435072 | tf_op jit(solution)/shard_map/vmap()/gather
  114.7 4.6 %dynamic-slice_dynamic-update-slice_fusion.2 = f32[4,259,1027]{2,1,0:T(8,128)} fusion(f32[4,259,1027]{2,1,0:T(8,128)} %get-tuple-element.118, s32[]{:T(128)} %get-tuple-element.115, f32[4,516,1284]{2,1,0:T(8,128)} %get-tuple-element.121, s32[]{:T(128)} %bitcast.84, s32[]{:T(128)} %bitcast.85, s32[]{:T(128)} %bitcast.86), kind=kLoop, calls=%fused_computation.clone.1 | loop fusion | bytes 2435072 | tf_op jit(solution)/shard_map/vmap()/gather
  120.0 4.7 %dynamic-slice_dynamic-update-slice_fusion.2 = f32[4,259,1027]{2,1,0:T(8,128)} fusion(f32[4,259,1027]{2,1,0:T(8,128)} %get-tuple-element.118, s32[]{:T(128)} %get-tuple-element.115, f32[4,516,1284]{2,1,0:T(8,128)} %get-tuple-element.121, s32[]{:T(128)} %bitcast.84, s32[]{:T(128)} %bitcast.85, s32[]{:T(128)} %bitcast.86), kind=kLoop, calls=%fused_computation.clone.1 | loop fusion | bytes 2435072 | tf_op jit(solution)/shard_map/vmap()/gather
  124.7 9.2 %multiply_add_fusion = f32[4,256,1027]{2,1,0:T(8,128)S(1)} fusion(f32[4,259,1027]{2,1,0:T(8,128)} %get-tuple-element.10, f32[4]{0:T(128)S(1)} %get-tuple-element.67, f32[4]{0:T(128)S(1)} %get-tuple-element.62, f32[4]{0:T(128)S(1)} %get-tuple-element.64, f32[4]{0:T(128)S(1)} %get-tuple-element.63), kind=kLoop, calls=%fused_computation.5 | loop fusion | flops 7361536 | bytes 21033024 | tf_op jit(solution)/shard_map/vmap()/add | solution.py:50
  133.9 3.4 fusion.25
  137.4 33.4 %collective-permute-start.4 = (f32[4,4,1024]{2,1,0:T(4,128)S(1)}, f32[4,4,1024]{2,1,0:T(4,128)S(1)}, u32[]{:S(2)}, u32[]{:S(2)}) collective-permute-start(f32[4,4,1024]{2,1,0:T(4,128)S(1)} %get-tuple-element.53), channel_id=1, source_target_pairs={{0,4},{4,8},{8,12},{12,16},{16,20},{20,24},{24,28},{1,5},{5,9},{9,... | collective-permute-start | bytes 196616 | tf_op jit(solution)/shard_map/ppermute | solution.py:28
  170.8 1.3 collective-permute-start.5
  172.1 16.2 %collective-permute-done.5 = f32[4,4,1024]{2,1,0:T(4,128)S(1)} collective-permute-done((f32[4,4,1024]{2,1,0:T(4,128)S(1)}, f32[4,4,1024]{2,1,0:T(4,128)S(1)}, u32[]{:S(2)}, u32[]{:S(2)}) %collective-permute-start.5) | collective-permute-done | bytes 65568 | tf_op jit(solution)/shard_map/ppermute | solution.py:29
  189.3 3.4 collective-permute-start.6
  193.0 1.5 collective-permute-start.7
  194.8 3.9 %collective-permute-done.7 = f32[4,264,4]{1,2,0:T(4,128)S(1)} collective-permute-done((f32[4,264,4]{1,2,0:T(4,128)S(1)}, f32[4,264,4]{1,2,0:T(4,128)S(1)}, u32[]{:S(2)}, u32[]{:S(2)}) %collective-permute-start.7) | collective-permute-done | bytes 16928 | tf_op jit(solution)/shard_map/ppermute | solution.py:29
  199.0 7.4 %maximum_maximum_fusion = (f32[4,264,1028]{2,1,0:T(8,128)S(1)}, f32[4,264,1028]{2,1,0:T(8,128)}) fusion(f32[4,4,1024]{2,1,0:T(4,128)S(1)} %collective-permute-done.5, f32[4,256,1024]{2,1,0:T(8,128)} %copy-done, f32[4,4,1024]{2,1,0:T(4,128)S(1)} %collective-permute-done.4, f32[4,264,4]{2,1,0:T(8,128)S(1)} %copy.33, f32[4,264,4]{2,1,0:T(8,128)S(1)} %copy.35), kind=kLoop, calls=%fused_computation.3 | loop fusion | flops 6513408 | bytes 13043712 | tf_op jit(solution)/shard_map/concatenate | solution.py:30
  206.4 15.3 %fusion.1 = f32[4,264,1024]{2,1,0:T(8,128)S(1)} fusion(f32[4,264,1028]{2,1,0:T(8,128)} %get-tuple-element.45, f32[4,264,1028]{2,1,0:T(8,128)S(1)} %get-tuple-element.44, f32[1024]{0:T(1024)S(1)} %fusion.76, f32[4,4,1024]{2,1,0:T(4,128)S(1)} %collective-permute-done.5, f32[4,256,1024]{2,1,0:T(8,128)} %copy-done, f32[4,4,1024]{2,1,0:T(4,128)S(1)} %collective-permute-done.4), kind=kLoop, calls=%fused_computation.8 | loop fusion | flops 20545536 | bytes 43257856 | tf_op jit(solution)/shard_map/div | solution.py:98
  221.7 5.7 %fusion.17 = f32[4,256,1024]{2,1,0:T(8,128)} fusion(f32[4,264,1024]{2,1,0:T(8,128)S(1)} %fusion.1, f32[256]{0:T(256)S(1)} %multiply_add_fusion.3), kind=kLoop, calls=%fused_computation.41 | loop fusion | flops 17825792 | bytes 41944064 | tf_op jit(solution)/shard_map/div | solution.py:108
  227.4 19.0 %reshape.249 = f32[4,16,16,64,16]{4,3,2,1,0:T(8,128)} reshape(f32[4,256,1024]{2,1,0:T(8,128)} %fusion.17) | data formatting | bytes 8388608 | tf_op jit(solution)/shard_map/reshape | solution.py:113
  246.4 12.2 %reduce_sum.45 = f32[4,16,64]{2,1,0:T(8,128)S(1)} reduce(f32[4,16,16,64,16]{4,3,2,1,0:T(8,128)} %reshape.249, f32[]{:T(128)} %constant.64.clone.1), dimensions={2,4}, to_apply=%region_0.0 | reduce | flops 1044480 | bytes 4210692 | tf_op jit(solution)/shard_map/reduce_sum | solution.py:113
  258.7 15.9 %all_gather.6 = f32[4,16,256]{1,0,2:T(4,128)S(1)} all-gather(f32[4,16,64]{1,0,2:T(4,128)S(1)} %copy.36), channel_id=1, replica_groups=mesh['row'=8,'col'=4] {'col'}, dimensions={2}, use_global_device_ids=true | all-gather | bytes 81920 | tf_op jit(solution)/shard_map/all_gather | solution.py:124
  275.6 10.9 %all_gather.7 = f32[4,128,64]{2,1,0:T(8,128)S(1)} all-gather(f32[4,16,64]{2,1,0:T(8,128)S(1)} %convolution_divide_fusion.1), channel_id=1, replica_groups=mesh['row'=8,'col'=4] {'row'}, dimensions={1}, use_global_device_ids=true | all-gather | bytes 147456 | tf_op jit(solution)/shard_map/all_gather | solution.py:135
  286.8 2.3 collective-permute-start.8
  289.1 1.3 collective-permute-start.9
  290.4 1.7 collective-permute-done.9
  292.2 1.3 collective-permute-start.10
  293.5 1.6 collective-permute-start.11
  295.3 4.3 %collective-permute-done.11 = f32[4,18,1]{2,1,0:T(8,128)S(1)} collective-permute-done((f32[4,18,1]{2,1,0:T(8,128)S(1)}, f32[4,18,1]{2,1,0:T(8,128)S(1)}, u32[]{:S(2)}, u32[]{:S(2)}) %collective-permute-start.11) | collective-permute-done | bytes 320 | tf_op jit(solution)/shard_map/ppermute | solution.py:29
  300.1 6.0 %convolution_subtract_fusion = f32[4,256,1024]{2,1,0:T(8,128)S(1)} fusion(f32[4,256,1024]{2,1,0:T(8,128)} %fusion.17, f32[4,256,66]{1,2,0:T(8,128)S(1)} %convolution_bitcast_fusion, f32[1024]{0:T(1024)S(1)} %get-tuple-element.71, s32[1024]{0:T(1024)S(1)} %get-tuple-element.74, f32[1024]{0:T(1024)S(1)} %get-tuple-element.72, ...), kind=kOutput, calls=%fused_computation.65 | convolution fusion | flops 831858688 | bytes 8675592 | tf_op jit(solution)/shard_map/spb,qb->spq/dot_general | solution.py:173
  306.1 2.6 collective-permute-start.12
  310.0 2.5 collective-permute-done.13
  313.0 1.3 collective-permute-start.14
  314.6 4.5 %collective-permute-start.15 = (f32[4,258,1]{1,0,2:T(4,128)S(1)}, f32[4,258,1]{1,0,2:T(4,128)S(1)}, u32[]{:S(2)}, u32[]{:S(2)}) collective-permute-start(f32[4,258,1]{1,0,2:T(4,128)S(1)} %copy.40), channel_id=1, source_target_pairs={{0,1},{1,2},{2,3},{4,5},{5,6},{6,7},{8,9},{9,10},{10,11},{12,13},{... | collective-permute-start | bytes 12392 | tf_op jit(solution)/shard_map/ppermute | solution.py:28
  320.7 13.9 %fusion.112 = (f32[4]{0:T(128)S(1)}, f32[4,256,1024]{2,1,0:T(8,128)}, f32[4]{0:T(128)S(1)}) fusion(f32[256]{0:T(256)S(1)} %and_convert_fusion, f32[4,256,1024]{2,1,0:T(8,128)} %copy-done.1, f32[4,1,1024]{2,1,0:T(1,128)S(1)} %collective-permute-done.12, f32[4,1,1024]{2,1,0:T(1,128)S(1)} %collective-permute-done.13, f32[1024]{0:T(1024)S(1)} %fusion.92, ...), kind=kLoop, calls=%fused_computation.219 | loop fusion | flops 18874360 | bytes 8434784 | tf_op jit(solution)/shard_map/reduce_sum | solution.py:206
  334.6 43.1 %all-reduce = (f32[1,4]{1,0:T(1,128)S(1)}, f32[1,4]{1,0:T(1,128)S(1)}) all-reduce(f32[1,4]{1,0:T(1,128)S(1)} %bitcast.87, f32[1,4]{1,0:T(1,128)S(1)} %bitcast.88), channel_id=1, replica_groups=mesh['row'=8,'col'=4] {'row','col'}, use_global_device_ids=true, to_apply=%region_6.7 | all-reduce | flops 8 | bytes 64 | tf_op jit(solution)/shard_map/psum | solution.py:207
  (74 shorter events, 11.6 us)
Async XLA Ops:
  5.3 13.3 %collective-permute-start = (f32[4,130,1024]{2,0,1:T(4,128)S(1)}, f32[4,130,1024]{2,0,1:T(4,128)}, u32[]{:S(2)}, u32[]{:S(2)}) collective-permute-start(f32[4,130,1024]{2,0,1:T(4,128)S(1)} %copy.42), channel_id=1, source_target_pairs={{0,4},{4,8},{8,12},{12,16},{16,20},{20,24},{24,28},{1,5},{5,9},{9,... | collective-permute-start | bytes 6389768 | tf_op jit(solution)/shard_map/ppermute | solution.py:28
  11.7 6.7 %copy-start.5 = (s32[2,4,1,1]{1,3,2,0:T(1,128)S(1)}, s32[2,4,1,1]{1,3,2,0:T(1,128)}, u32[]{:S(2)}) copy-start(s32[2,4,1,1]{1,3,2,0:T(1,128)} %param.6) | copy-start | bytes 100
  11.7 13.1 %collective-permute-start.1 = (f32[4,130,1024]{2,0,1:T(4,128)}, f32[4,130,1024]{2,0,1:T(4,128)}, u32[]{:S(2)}, u32[]{:S(2)}) collective-permute-start(f32[4,130,1024]{2,0,1:T(4,128)} %copy.43), channel_id=1, source_target_pairs={{4,0},{8,4},{12,8},{16,12},{20,16},{24,20},{28,24},{5,1},{9,5},{13... | collective-permute-start | bytes 6389768 | tf_op jit(solution)/shard_map/ppermute | solution.py:29
  31.0 9.9 %copy-start.4 = (s32[2,4,1,1]{1,3,2,0:T(1,128)S(1)}, s32[2,4,1,1]{1,3,2,0:T(1,128)}, u32[]{:S(2)}) copy-start(s32[2,4,1,1]{1,3,2,0:T(1,128)} %param.7) | copy-start | bytes 100
  31.0 27.6 %copy-start.2 = (f32[4,256,1024]{1,0,2:T(4,128)S(1)}, f32[4,256,1024]{1,0,2:T(4,128)}, u32[]{:S(2)}) copy-start(f32[4,256,1024]{1,0,2:T(4,128)} %copy.28) | copy-start | bytes 12582916
  34.5 19.6 %collective-permute-start.2 = (f32[4,516,130]{1,0,2:T(4,128)S(1)}, f32[4,516,130]{1,0,2:T(4,128)S(1)}, u32[]{:S(2)}, u32[]{:S(2)}) collective-permute-start(f32[4,516,130]{1,0,2:T(4,128)S(1)} %get-tuple-element.42), channel_id=1, source_target_pairs={{0,1},{1,2},{2,3},{4,5},{5,6},{6,7},{8,9},{9,10},{10,11},{12,13},{... | collective-permute-start | bytes 3219848 | tf_op jit(solution)/shard_map/ppermute | solution.py:28
  38.9 19.7 %collective-permute-start.3 = (f32[4,516,130]{1,0,2:T(4,128)S(1)}, f32[4,516,130]{1,0,2:T(4,128)S(1)}, u32[]{:S(2)}, u32[]{:S(2)}) collective-permute-start(f32[4,516,130]{1,0,2:T(4,128)S(1)} %get-tuple-element.43), channel_id=1, source_target_pairs={{1,0},{2,1},{3,2},{5,4},{6,5},{7,6},{9,8},{10,9},{11,10},{13,12},{... | collective-permute-start | bytes 3219848 | tf_op jit(solution)/shard_map/ppermute | solution.py:29
  124.7 9.2 %copy-start.3 = (f32[4,256,1024]{2,1,0:T(8,128)S(1)}, f32[4,256,1024]{2,1,0:T(8,128)}, u32[]{:S(2)}) copy-start(f32[4,256,1024]{2,1,0:T(8,128)} %param.4) | copy-start | bytes 12582916
  137.3 51.5 %copy-start = (f32[4,256,1024]{2,1,0:T(8,128)}, f32[4,256,1024]{2,1,0:T(8,128)S(1)}, u32[]{:S(2)}) copy-start(f32[4,256,1024]{2,1,0:T(8,128)S(1)} %fusion.25) | copy-start | bytes 12582916
  137.4 34.7 %collective-permute-start.4 = (f32[4,4,1024]{2,1,0:T(4,128)S(1)}, f32[4,4,1024]{2,1,0:T(4,128)S(1)}, u32[]{:S(2)}, u32[]{:S(2)}) collective-permute-start(f32[4,4,1024]{2,1,0:T(4,128)S(1)} %get-tuple-element.53), channel_id=1, source_target_pairs={{0,4},{4,8},{8,12},{12,16},{16,20},{20,24},{24,28},{1,5},{5,9},{9,... | collective-permute-start | bytes 196616 | tf_op jit(solution)/shard_map/ppermute | solution.py:28
  170.8 17.5 %collective-permute-start.5 = (f32[4,4,1024]{2,1,0:T(4,128)S(1)}, f32[4,4,1024]{2,1,0:T(4,128)S(1)}, u32[]{:S(2)}, u32[]{:S(2)}) collective-permute-start(f32[4,4,1024]{2,1,0:T(4,128)S(1)} %get-tuple-element.54), channel_id=1, source_target_pairs={{4,0},{8,4},{12,8},{16,12},{20,16},{24,20},{28,24},{5,1},{9,5},{13... | collective-permute-start | bytes 196616 | tf_op jit(solution)/shard_map/ppermute | solution.py:29
  189.3 5.2 %collective-permute-start.6 = (f32[4,264,4]{1,2,0:T(4,128)S(1)}, f32[4,264,4]{1,2,0:T(4,128)S(1)}, u32[]{:S(2)}, u32[]{:S(2)}) collective-permute-start(f32[4,264,4]{1,2,0:T(4,128)S(1)} %copy.32), channel_id=1, source_target_pairs={{0,1},{1,2},{2,3},{4,5},{5,6},{6,7},{8,9},{9,10},{10,11},{12,13},{... | collective-permute-start | bytes 50696 | tf_op jit(solution)/shard_map/ppermute | solution.py:28
  193.0 5.7 %collective-permute-start.7 = (f32[4,264,4]{1,2,0:T(4,128)S(1)}, f32[4,264,4]{1,2,0:T(4,128)S(1)}, u32[]{:S(2)}, u32[]{:S(2)}) collective-permute-start(f32[4,264,4]{1,2,0:T(4,128)S(1)} %copy.34), channel_id=1, source_target_pairs={{1,0},{2,1},{3,2},{5,4},{6,5},{7,6},{9,8},{10,9},{11,10},{13,12},{... | collective-permute-start | bytes 50696 | tf_op jit(solution)/shard_map/ppermute | solution.py:29
  286.8 3.6 collective-permute-start.8
  289.1 3.1 collective-permute-start.9
  292.2 3.1 collective-permute-start.10
  293.5 6.0 %collective-permute-start.11 = (f32[4,18,1]{2,1,0:T(8,128)S(1)}, f32[4,18,1]{2,1,0:T(8,128)S(1)}, u32[]{:S(2)}, u32[]{:S(2)}) collective-permute-start(f32[4,18,1]{2,1,0:T(8,128)S(1)} %get-tuple-element.58), channel_id=1, source_target_pairs={{1,0},{2,1},{3,2},{5,4},{6,5},{7,6},{9,8},{10,9},{11,10},{13,12},{... | collective-permute-start | bytes 872 | tf_op jit(solution)/shard_map/ppermute | solution.py:29
  306.1 6.5 %copy-start.1 = (f32[4,256,1024]{2,1,0:T(8,128)}, f32[4,256,1024]{2,1,0:T(8,128)S(1)}, u32[]{:S(2)}) copy-start(f32[4,256,1024]{2,1,0:T(8,128)S(1)} %convolution_subtract_fusion) | copy-start | bytes 12582916
  306.1 3.9 %collective-permute-start.12 = (f32[4,1,1024]{2,1,0:T(1,128)S(1)}, f32[4,1,1024]{2,1,0:T(1,128)S(1)}, u32[]{:S(2)}, u32[]{:S(2)}) collective-permute-start(f32[4,1,1024]{2,1,0:T(1,128)S(1)} %get-tuple-element.52), channel_id=1, source_target_pairs={{0,4},{4,8},{8,12},{12,16},{16,20},{20,24},{24,28},{1,5},{5,9},{9,... | collective-permute-start | bytes 49160 | tf_op jit(solution)/shard_map/ppermute | solution.py:28
  308.7 3.8 %collective-permute-start.13 = (f32[4,1,1024]{2,1,0:T(1,128)S(1)}, f32[4,1,1024]{2,1,0:T(1,128)S(1)}, u32[]{:S(2)}, u32[]{:S(2)}) collective-permute-start(f32[4,1,1024]{2,1,0:T(1,128)S(1)} %get-tuple-element.51), channel_id=1, source_target_pairs={{4,0},{8,4},{12,8},{16,12},{20,16},{24,20},{28,24},{5,1},{9,5},{13... | collective-permute-start | bytes 49160 | tf_op jit(solution)/shard_map/ppermute | solution.py:29
  313.0 6.1 %collective-permute-start.14 = (f32[4,258,1]{1,0,2:T(4,128)S(1)}, f32[4,258,1]{1,0,2:T(4,128)S(1)}, u32[]{:S(2)}, u32[]{:S(2)}) collective-permute-start(f32[4,258,1]{1,0,2:T(4,128)S(1)} %copy.38), channel_id=1, source_target_pairs={{1,0},{2,1},{3,2},{5,4},{6,5},{7,6},{9,8},{10,9},{11,10},{13,12},{... | collective-permute-start | bytes 12392 | tf_op jit(solution)/shard_map/ppermute | solution.py:29
  314.6 5.9 %collective-permute-start.15 = (f32[4,258,1]{1,0,2:T(4,128)S(1)}, f32[4,258,1]{1,0,2:T(4,128)S(1)}, u32[]{:S(2)}, u32[]{:S(2)}) collective-permute-start(f32[4,258,1]{1,0,2:T(4,128)S(1)} %copy.40), channel_id=1, source_target_pairs={{0,1},{1,2},{2,3},{4,5},{5,6},{6,7},{8,9},{9,10},{10,11},{12,13},{... | collective-permute-start | bytes 12392 | tf_op jit(solution)/shard_map/ppermute | solution.py:28
where the time goes:
time: 380 us; the launch traced here: 378 us
  other arithmetic  102 us (27%)
  local copies, waits for them, and re-layouts  83.1 us (22%)
  blocking collectives  69.9 us (18%)
  starting transfers between devices  66.8 us (18%)
  waiting for transfers between devices  47.5 us (12%)
  matrix products  7.8 us (2%)
    ppermute x8, starting transfers between devices, with_halo(): before = lax.ppermute(last, axis, up)  55.6 us
    psum x1, blocking collectives, body(): height_all, slope_all = lax.psum((height_sq, slope_sum), ('row', 'col'))  43.1 us
    concatenate x4, other arithmetic, with_halo(): value = jnp.concatenate([before, value, after], axis=dim)  37.5 us
    ppermute x8, waiting for transfers between devices, with_halo(): after = lax.ppermute(leading, axis, down)  33.1 us
    unnamed x18, local copies, waits for them, and re-layouts  24.7 us
    gather x12, local copies, waits for them, and re-layouts  21.3 us
    reshape x1, local copies, waits for them, and re-layouts, coarse_means(): surface.reshape(scans, height // BLOCK, BLOCK, length // BLOCK, BLOCK)  19 us
    all_gather x1, blocking collectives, long_cols(): portion = lax.all_gather(coarse, 'col', axis=2, tiled=True)  15.9 us
  transfers between devices with their start and end apart: 16, of which 9 were waited for; matrix products, arithmetic and copies ran while one was open for 4% of the time, Pallas kernels for 0%

commit v1 on v0

v1 whole, which is shorter than its diff:
```python
import functools
import math

import jax
import jax.numpy as jnp
import numpy as np
from jax import lax
from jax.experimental import pallas as pl
from jax.experimental.pallas import tpu as pltpu
from jax.sharding import PartitionSpec as P

LS = 5
SR = 4
LCUT = 1600
BLOCK = 16
DRIFT = 128
EPSILON = 1e-06
ALPHA = math.sqrt(math.log(2.0) / math.pi)
TAPS = [math.exp(-math.pi * (k / (ALPHA * LS)) ** 2) for k in range(-SR, SR + 1)]
HALO = 136
LANES = 128
EDGE = 8
F32 = jnp.float32
BF16 = jnp.bfloat16
HIGHEST = lax.Precision.HIGHEST
MESH = pl.DeviceIdType.MESH
ANY = pl.BlockSpec(memory_space=pl.ANY)
VM = pl.BlockSpec(memory_space=pltpu.VMEM)
VMEM_LIMIT = 56 * 1024 * 1024


def short_matrix(count):
    index = np.arange(count)
    matrix = np.zeros((count, count), np.float64)
    for k in range(-SR, SR + 1):
        rows = index[(index + k >= 0) & (index + k < count)]
        matrix[rows, rows + k] = TAPS[k + SR]
    return matrix, matrix.sum(axis=1)


def coarse_table(count, tile, padded):
    parts = count // tile
    blocks = tile // BLOCK
    _, weight = short_matrix(count)
    table = np.zeros((parts, padded, tile), np.float64)
    for part in range(parts):
        for b in range(-1, blocks + 1):
            target = part * blocks + b
            if target < 0 or target >= count // BLOCK:
                continue
            for p in range(target * BLOCK, (target + 1) * BLOCK):
                for k in range(-SR, SR + 1):
                    source = p + k - part * tile
                    if 0 <= source < tile:
                        table[part, b + 1, source] += TAPS[k + SR] / weight[p] / BLOCK
    return table


def long_matrix(blocks):
    index = np.arange(blocks)
    distance = (index[:, None] - index[None, :]) * BLOCK / (ALPHA * LCUT)
    matrix = np.exp(-math.pi * distance * distance)
    return matrix / matrix.sum(axis=1, keepdims=True)


def upsample_rows(count, first, length):
    blocks = count // BLOCK
    result = np.zeros((length, blocks), np.float64)
    for n in range(length):
        p = first + n
        if p < 0 or p >= count:
            continue
        u = (2 * p + 1 - BLOCK) / (2 * BLOCK)
        i = math.floor(u)
        f = u - i
        if i < 0:
            i, f = 0, 0.0
        if i >= blocks - 1:
            i, f = blocks - 1, 0.0
        result[n, i] += 1 - f
        if f:
            result[n, i + 1] += f
    return result


def spread_table(count, tile, padded):
    parts, blocks = count // tile, tile // BLOCK
    total = count // BLOCK
    table = np.zeros((total, parts, padded), np.float64)
    matrix = long_matrix(total)
    for part in range(parts):
        for b in range(-1, blocks + 1):
            source = part * blocks + b
            if 0 <= source < total:
                table[:, part, b + 1] = matrix[:, source]
    return table


@functools.lru_cache(maxsize=None)
def tables(nr, nc, tr, tc):
    n_row, n_col = nr // tr, nc // tc
    br, bc = tr // BLOCK, tc // BLOCK
    pr = -(-(br + 2) // 8) * 8
    r_table = coarse_table(nr, tr, pr)
    c_table = coarse_table(nc, tc, LANES).transpose(0, 2, 1)
    col_spread = spread_table(nc, tc, LANES)
    hc = np.zeros((n_col, n_col, LANES, LANES))
    cu = np.zeros((n_col, LANES, tc + 2 * LANES))
    for part in range(n_col):
        for b in range(-1, bc + 1):
            target = part * bc + b
            if 0 <= target < nc // BLOCK:
                hc[part, :, :, b + 1] = col_spread[target]
        up = upsample_rows(nc, part * tc - LANES, tc + 2 * LANES)
        for b in range(-1, bc + 1):
            target = part * bc + b
            if 0 <= target < nc // BLOCK:
                cu[part, b + 1] = up[:, target]
    row_spread = spread_table(nr, tr, pr).reshape(nr // BLOCK, n_row * pr)
    ru = np.stack(
        [upsample_rows(nr, part * tr - EDGE, tr + 2 * EDGE) @ row_spread for part in range(n_row)]
    )
    _, row_weight = short_matrix(nr)
    _, col_weight = short_matrix(nc)
    rw = np.zeros((n_row, tr + 2 * EDGE, 1))
    cw = np.zeros((n_col, 1, tc + 2 * LANES))
    for part in range(n_row):
        for n in range(tr + 2 * EDGE):
            p = part * tr - EDGE + n
            if 0 <= p < nr:
                rw[part, n, 0] = 1.0 / row_weight[p]
    for part in range(n_col):
        for n in range(tc + 2 * LANES):
            q = part * tc - LANES + n
            if 0 <= q < nc:
                cw[part, 0, n] = 1.0 / col_weight[q]
    return [t.astype(np.float32) for t in (r_table, c_table, hc, cu, ru, rw, cw)]


def remote(src, dst, send, recv, device):
    return pltpu.make_async_remote_copy(
        src_ref=src, dst_ref=dst, send_sem=send, recv_sem=recv,
        device_id=device, device_id_type=MESH,
    )


def signal(barrier, device):
    pl.semaphore_signal(barrier, inc=1, device_id=device, device_id_type=MESH)


def neighbours(n_row, n_col):
    row, col = lax.axis_index("row"), lax.axis_index("col")
    found = {}
    for dr in (-1, 0, 1):
        for dc in (-1, 0, 1):
            if dr == 0 and dc == 0:
                continue
            r, c = row + dr, col + dc
            exists = (r >= 0) & (r < n_row) & (c >= 0) & (c < n_col)
            found[dr, dc] = (exists, (r, c))
    return found


def halo_kernel(n_row, n_col, after, extra, wide, slots, own_sem, send, recv, slot_send, slot_recv):
    scans, height, length = after.shape
    near = neighbours(n_row, n_col)
    barrier = pltpu.get_barrier_semaphore()
    count = jnp.int32(0)
    for exists, device in near.values():
        count += exists.astype(jnp.int32)

        @pl.when(exists)
        def _():
            signal(barrier, device)

    pl.semaphore_wait(barrier, count)
    low, high = HALO, HALO + height
    bands = {-1: (0, HALO), 0: (low, height), 1: (high, HALO)}
    mid = pl.ds(LANES, length)

    def row_copy(s, dr):
        src = pl.ds(height - HALO, HALO) if dr == 1 else pl.ds(0, HALO)
        dst = pl.ds(0, HALO) if dr == 1 else pl.ds(high, HALO)
        k = 0 if dr == 1 else 1
        return remote(
            after.at[s, src, :], wide.at[s, dst, mid], send.at[k, s], recv.at[k, s], near[dr, 0][1]
        )

    def col_copy(s, dc, band):
        start, rows = bands[band]
        k = 2 + (band + 1) * 2 + (0 if dc == 1 else 1)
        first = length - LANES if dc == 1 else 0
        if band == 0:
            src = after.at[s, :, pl.ds(first, LANES)]
        else:
            src = wide.at[s, pl.ds(start, rows), pl.ds(LANES + first, LANES)]
        dst = wide.at[s, pl.ds(start, rows), pl.ds(0 if dc == 1 else LANES + length, LANES)]
        return remote(src, dst, send.at[k, s], recv.at[k, s], near[0, dc][1])

    def slot_copy(dr, dc):
        k = (0 if dc == 1 else 3) + (1 - dr)
        return remote(extra, slots.at[k], slot_send.at[k], slot_recv.at[k], near[dr, dc][1])

    def when(pred, action):
        pl.when(pred)(action)

    for s in range(scans):
        for dr in (1, -1):
            when(near[dr, 0][0], row_copy(s, dr).start)
    for s in range(scans):
        for dc in (1, -1):
            when(near[0, dc][0], col_copy(s, dc, 0).start)
    own = pltpu.make_async_copy(after, wide.at[:, pl.ds(low, height), mid], own_sem)
    own.start()
    for dc in (1, -1):
        for dr in (-1, 0, 1):
            when(near[dr, dc][0], slot_copy(dr, dc).start)
    for s in range(scans):
        for dr in (1, -1):
            source = near[-dr, 0][0]
            when(source, row_copy(s, dr).wait_recv)
            for dc in (1, -1):
                when(source & near[0, dc][0], col_copy(s, dc, -dr).start)
    for s in range(scans):
        for dr in (1, -1):
            when(near[dr, 0][0], row_copy(s, dr).wait_send)
        for dc in (1, -1):
            for band in (-1, 0, 1):
                ok = jnp.bool_(True) if band == 0 else near[band, 0][0]
                when(ok & near[0, dc][0], col_copy(s, dc, band).wait_send)
                when(ok & near[0, -dc][0], col_copy(s, dc, band).wait_recv)
    for dc in (1, -1):
        for dr in (-1, 0, 1):
            when(near[dr, dc][0], slot_copy(dr, dc).wait_send)
            when(near[-dr, -dc][0], slot_copy(dr, dc).wait_recv)
    own.wait()


def split3(value):
    a = value.astype(BF16)
    rest = value - a.astype(F32)
    b = rest.astype(BF16)
    c = (rest - b.astype(F32)).astype(BF16)
    return a, b, c


def cubic(t):
    t2 = t * t
    t3 = t2 * t
    return (
        0.5 * (2.0 * t2 - t3 - t),
        0.5 * (3.0 * t3 - 5.0 * t2 + 2.0),
        0.5 * (4.0 * t2 - 3.0 * t3 + t),
        0.5 * (t3 - t2),
    )


def shift_kernel(place, offsets, fractions, wide, before, slots, r_tab, c_tab, diff, partial, edges, tail):
    s = pl.program_id(0)
    height, length = before.shape[1], before.shape[2]
    total = length + 3 * LANES
    dr, dc = offsets[0, s], offsets[1, s]
    rt = cubic(fractions[0, s].astype(F32) / 256.0)
    ct = cubic(fractions[1, s].astype(F32) / 256.0)
    blank = jnp.zeros((LANES - 16, height), F32)
    for j in range(3):
        block = jnp.concatenate([slots[3 + j, 0], blank, slots[j, 0]], axis=0)
        flipped = jnp.transpose(block)
        if j == 0:
            tail[0:HALO] = flipped[height - HALO :]
        elif j == 1:
            tail[HALO : HALO + height] = flipped
        else:
            tail[HALO + height :] = flipped[:HALO]
    turn = 2 * total - LANES - dc + 1
    turn = lax.rem(turn, total)
    start = HALO - 1 + dr
    rows = 32

    def step(r, carry):
        first = start + r * rows
        base = pl.multiple_of((first // 8) * 8, 8)
        off = first - base
        x = jnp.concatenate(
            [wide[0, pl.ds(base, rows + 16), :], tail[pl.ds(base, rows + 16), :]], axis=1
        )
        x = pltpu.roll(x, lax.rem(rows + 16 - off, rows + 16), 0)
        y = rt[0] * x[0:rows] + rt[1] * x[1 : rows + 1] + rt[2] * x[2 : rows + 2] + rt[3] * x[3 : rows + 3]
        y = pltpu.roll(y, turn, 1)
        z = ct[0] * y[:, 0:length]
        for b in range(1, 4):
            z = z + ct[b] * pltpu.roll(y, total - b, 1)[:, 0:length]
        here = pl.ds(pl.multiple_of(r * rows, rows), rows)
        diff[0, here, :] = before[0, here, :] - z
        return carry

    lax.fori_loop(0, height // rows, step, 0)
    d = diff[0]
    mixed = jnp.dot(r_tab[0], d, precision=HIGHEST, preferred_element_type=F32)
    partial[0] = jnp.dot(mixed, c_tab[0], precision=HIGHEST, preferred_element_type=F32)
    edges[0, 0:EDGE] = jnp.transpose(diff[0, :, 0:LANES])[0:EDGE]
    edges[0, EDGE:] = jnp.transpose(diff[0, :, length - LANES :])[LANES - EDGE :]


def gather_kernel(n_row, n_col, diff, partial, edges, hc, rows_out, corners, sides, spread, parts,
                  psend, precv, qsend, qrecv, nsend, nrecv):
    scans, height, length = diff.shape
    near = neighbours(n_row, n_col)
    row, col = lax.axis_index("row"), lax.axis_index("col")
    barrier = pltpu.get_barrier_semaphore()
    count = jnp.int32(n_row - 1 + n_col - 1)
    for k in range(1, n_col):
        signal(barrier, (row, lax.rem(col + k, n_col)))
    for k in range(1, n_row):
        signal(barrier, (lax.rem(row + k, n_row), col))
    for (dr, dc), (exists, device) in near.items():
        if dr and dc:
            count += exists.astype(jnp.int32)

            @pl.when(exists)
            def _():
                signal(barrier, device)

    pl.semaphore_wait(barrier, count)

    def p_copy(k):
        return remote(
            partial, parts.at[col], psend.at[k - 1], precv.at[k - 1], (row, lax.rem(col + k, n_col))
        )

    def q_copy(k):
        return remote(
            spread.at[row], spread.at[row], qsend.at[k - 1], qrecv.at[k - 1],
            (lax.rem(row + k, n_row), col),
        )

    def near_copy(dr, dc):
        device = near[dr, dc][1]
        vertical = pl.ds(height - EDGE, EDGE) if dr == 1 else pl.ds(0, EDGE)
        k = (dr + 1) * 3 + dc + 1
        v = 0 if dr == 1 else 1
        if dc == 0:
            src, dst = diff.at[:, vertical, :], rows_out.at[v]
        elif dr == 0:
            src = edges.at[:, pl.ds(EDGE if dc == 1 else 0, EDGE), :]
            dst = sides.at[0 if dc == 1 else 1]
        else:
            lanes = pl.ds(length - LANES, LANES) if dc == 1 else pl.ds(0, LANES)
            src = diff.at[:, vertical, lanes]
            dst = corners.at[v * 2 + (0 if dc == 1 else 1)]
        return remote(src, dst, nsend.at[k], nrecv.at[k], device)

    for k in range(1, n_col):
        p_copy(k).start()
    for (dr, dc), (exists, _) in near.items():
        pl.when(exists)(near_copy(dr, dc).start)
    own = [
        jnp.dot(partial[s], hc[0, col], precision=HIGHEST, preferred_element_type=F32)
        for s in range(scans)
    ]
    for k in range(1, n_col):
        p_copy(k).wait_recv()
        source = lax.rem(col - k + n_col, n_col)
        for s in range(scans):
            own[s] = own[s] + jnp.dot(
                parts[source, s], hc[0, source], precision=HIGHEST, preferred_element_type=F32
            )
    for s in range(scans):
        spread[row, s] = own[s]
    for k in range(1, n_row):
        q_copy(k).start()
    for k in range(1, n_col):
        p_copy(k).wait_send()
    for (dr, dc), (exists, _) in near.items():
        pl.when(exists)(near_copy(dr, dc).wait_send)
        pl.when(near[-dr, -dc][0])(near_copy(dr, dc).wait_recv)
    for k in range(1, n_row):
        q_copy(k).wait_send()
        q_copy(k).wait_recv()


def band_kernel(n_row, n_col, place, diff, rows_in, corners, sides, spread, ru, cu, rw, cw,
                band_out, slope_out, sums, x, a, b):
    row, col = place[0], place[1]
    height, length = diff.shape[1], diff.shape[2]
    width = length + 2 * LANES
    tall = height + 2 * EDGE
    zero = jnp.float32(0.0)
    has_top, has_bottom = row > 0, row < n_row - 1
    has_left, has_right = col > 0, col < n_col - 1
    mid = slice(LANES, LANES + length)
    x[EDGE : EDGE + height, mid] = diff[0]
    x[0:EDGE, mid] = jnp.where(has_top, rows_in[0, 0], zero)
    x[EDGE + height :, mid] = jnp.where(has_bottom, rows_in[1, 0], zero)
    x[0:EDGE, 0:LANES] = jnp.where(has_top & has_left, corners[0, 0], zero)
    x[0:EDGE, LANES + length :] = jnp.where(has_top & has_right, corners[1, 0], zero)
    x[EDGE + height :, 0:LANES] = jnp.where(has_bottom & has_left, corners[2, 0], zero)
    x[EDGE + height :, LANES + length :] = jnp.where(has_bottom & has_right, corners[3, 0], zero)
    blank = jnp.zeros((LANES - EDGE, height), F32)
    left = jnp.where(has_left, sides[0, 0], zero)
    right = jnp.where(has_right, sides[1, 0], zero)
    x[EDGE : EDGE + height, 0:LANES] = jnp.transpose(jnp.concatenate([blank, left], axis=0))
    x[EDGE : EDGE + height, LANES + length :] = jnp.transpose(
        jnp.concatenate([right, blank], axis=0)
    )

    def across(r, carry):
        here = pl.ds(pl.multiple_of(r * 16, 16), 16)
        v = x[here, :]
        total = TAPS[SR] * v
        for k in range(1, SR + 1):
            total = total + TAPS[SR + k] * (pltpu.roll(v, k, 1) + pltpu.roll(v, width - k, 1))
        a[here, :] = total * cw[0]
        return carry

    lax.fori_loop(0, tall // 16, across, 0)
    q = jnp.concatenate([spread[i, 0] for i in range(n_row)], axis=0)
    mixed = jnp.dot(ru[0], q, precision=HIGHEST, preferred_element_type=F32)
    pieces = jnp.concatenate(split3(mixed), axis=1)
    cub = cu[0].astype(BF16)
    wavy = jnp.dot(pieces, jnp.concatenate([cub, cub, cub], axis=0), preferred_element_type=F32)
    b[...] = wavy

    def along(r, carry):
        base = pl.multiple_of(r * 8, 8)
        v = a[pl.ds(base, 24), :]
        total = TAPS[SR] * v[8:16]
        for k in range(1, SR + 1):
            total = total + TAPS[SR + k] * (v[8 - k : 16 - k] + v[8 + k : 16 + k])
        here = pl.ds(base + 8, 8)
        b[here, :] = total * rw[0, here, :] - b[here, :]
        return carry

    lax.fori_loop(0, height // 8, along, 0)
    for edge in (EDGE - 1, EDGE + height):
        total = TAPS[SR] * a[edge : edge + 1, :]
        for k in range(1, SR + 1):
            total = total + TAPS[SR + k] * (
                a[edge - k : edge - k + 1, :] + a[edge + k : edge + k + 1, :]
            )
        b[edge : edge + 1, :] = total * rw[0, edge : edge + 1, :] - b[edge : edge + 1, :]

    lane = lax.broadcasted_iota(jnp.int32, (1, length), 1) + col * length
    col_mask = ((lane >= 1) & (lane <= n_col * length - 2)).astype(F32)

    def slope(r, carry):
        base = pl.multiple_of(r * 8, 8)
        v = b[pl.ds(base, 24), :]
        center = v[8:16]
        gc = (pltpu.roll(center, width - 1, 1) - pltpu.roll(center, 1, 1))[:, mid] * col_mask
        index = lax.broadcasted_iota(jnp.int32, (8, 1), 0) + row * height + base
        row_mask = ((index >= 1) & (index <= n_row * height - 2)).astype(F32)
        gr = (v[9:17, mid] - v[7:15, mid]) * row_mask
        value = gc * gc + gr * gr
        field = center[:, mid]
        here = pl.ds(base, 8)
        band_out[0, here, :] = field
        slope_out[0, here, :] = value
        return carry[0] + field * field, carry[1] + value

    start = jnp.zeros((8, length), F32)
    heights, slopes = lax.fori_loop(0, height // 8, slope, (start, start))
    sums[0, 0] = sum(heights[:, i : i + LANES] for i in range(0, length, LANES))
    sums[0, 1] = sum(slopes[:, i : i + LANES] for i in range(0, length, LANES))


def body(n_row, n_col, before, after, offsets, fractions):
    scans, height, length = before.shape
    width = length + 2 * LANES
    tall = height + 2 * EDGE
    r_tab, c_tab, hc, cu, ru, rw, cw = tables(n_row * height, n_col * length, height, length)
    pr = r_tab.shape[1]
    place = jnp.stack([lax.axis_index("row"), lax.axis_index("col")]).astype(jnp.int32)
    filler = jnp.zeros((scans, height, 5), F32)
    extra = jnp.concatenate(
        [after[:, :, LANES : LANES + 2], filler, after[:, :, length - LANES - 1 : length - LANES]], axis=2
    ).transpose(0, 2, 1)
    struct = jax.ShapeDtypeStruct
    dma = pltpu.SemaphoreType.DMA
    wide, slots = pl.pallas_call(
        functools.partial(halo_kernel, n_row, n_col),
        out_shape=(
            struct((scans, height + 2 * HALO, width), F32),
            struct((6, scans, 8, height), F32),
        ),
        in_specs=[ANY, ANY],
        out_specs=(ANY, ANY),
        scratch_shapes=[dma, dma((8, scans)), dma((8, scans)), dma((6,)), dma((6,))],
        compiler_params=pltpu.CompilerParams(
            collective_id=0, has_side_effects=True, vmem_limit_bytes=VMEM_LIMIT
        ),
        name="halo",
    )(after, extra)

    by_scan = lambda s, *_: (s, 0, 0)
    row_part = lambda s, p, *_: (p[0], 0, 0)
    col_part = lambda s, p, *_: (p[1], 0, 0)
    diff, partial, edges = pl.pallas_call(
        shift_kernel,
        out_shape=(
            struct((scans, height, length), F32),
            struct((scans, pr, LANES), F32),
            struct((scans, 2 * EDGE, height), F32),
        ),
        grid_spec=pltpu.PrefetchScalarGridSpec(
            num_scalar_prefetch=3,
            grid=(scans,),
            in_specs=[
                pl.BlockSpec((1, height + 2 * HALO, width), by_scan),
                pl.BlockSpec((1, height, length), by_scan),
                pl.BlockSpec((6, 1, 8, height), lambda s, *_: (0, s, 0, 0)),
                pl.BlockSpec((1, pr, height), row_part),
                pl.BlockSpec((1, length, LANES), col_part),
            ],
            out_specs=(
                pl.BlockSpec((1, height, length), by_scan),
                pl.BlockSpec((1, pr, LANES), by_scan),
                pl.BlockSpec((1, 2 * EDGE, height), by_scan),
            ),
            scratch_shapes=[pltpu.VMEM((height + 2 * HALO, LANES), F32)],
        ),
        compiler_params=pltpu.CompilerParams(vmem_limit_bytes=VMEM_LIMIT),
        name="shift",
    )(place, offsets[:, :, 0, 0], fractions[:, :, 0, 0], wide, before, slots, r_tab, c_tab)

    hc_here = lax.dynamic_index_in_dim(jnp.asarray(hc), place[1], 0, keepdims=True)
    rows_out, corners, sides, spread = pl.pallas_call(
        functools.partial(gather_kernel, n_row, n_col),
        out_shape=(
            struct((2, scans, EDGE, length), F32),
            struct((4, scans, EDGE, LANES), F32),
            struct((2, scans, EDGE, height), F32),
            struct((n_row, scans, pr, LANES), F32),
        ),
        in_specs=[ANY, VM, VM, VM],
        out_specs=(VM, VM, VM, VM),
        scratch_shapes=[
            pltpu.VMEM((n_col, scans, pr, LANES), F32),
            dma((n_col - 1,)), dma((n_col - 1,)), dma((n_row - 1,)), dma((n_row - 1,)),
            dma((9,)), dma((9,)),
        ],
        compiler_params=pltpu.CompilerParams(
            collective_id=1, has_side_effects=True, vmem_limit_bytes=VMEM_LIMIT
        ),
        name="gather",
    )(diff, partial, edges, hc_here)

    all_scan = lambda s, *_: (0, s, 0, 0)
    band, slope, sums = pl.pallas_call(
        functools.partial(band_kernel, n_row, n_col),
        out_shape=(
            struct((scans, height, length), F32),
            struct((scans, height, length), F32),
            struct((scans, 2, 8, LANES), F32),
        ),
        grid_spec=pltpu.PrefetchScalarGridSpec(
            num_scalar_prefetch=1,
            grid=(scans,),
            in_specs=[
                pl.BlockSpec((1, height, length), by_scan),
                pl.BlockSpec((2, 1, EDGE, length), all_scan),
                pl.BlockSpec((4, 1, EDGE, LANES), all_scan),
                pl.BlockSpec((2, 1, EDGE, height), all_scan),
                pl.BlockSpec((n_row, 1, pr, LANES), all_scan),
                pl.BlockSpec((1, tall, n_row * pr), row_part),
                pl.BlockSpec((1, LANES, width), col_part),
                pl.BlockSpec((1, tall, 1), row_part),
                pl.BlockSpec((1, 1, width), col_part),
            ],
            out_specs=(
                pl.BlockSpec((1, height, length), by_scan),
                pl.BlockSpec((1, height, length), by_scan),
                pl.BlockSpec((1, 2, 8, LANES), lambda s, *_: (s, 0, 0, 0)),
            ),
            scratch_shapes=[pltpu.VMEM((tall, width), F32)] * 3,
        ),
        compiler_params=pltpu.CompilerParams(vmem_limit_bytes=VMEM_LIMIT),
        name="band",
    )(place, diff, rows_out, corners, sides, spread, ru, cu, rw, cw)
    totals = lax.psum(jnp.sum(sums, axis=(2, 3)).T, ("row", "col"))
    cells = n_row * height * n_col * length
    return band, slope, jnp.sqrt(totals / cells + EPSILON)


def solution(mesh):
    n_row, n_col = mesh.shape["row"], mesh.shape["col"]
    spec = P(None, "row", "col")
    small = P(None, None, "row", "col")
    return jax.shard_map(
        functools.partial(body, n_row, n_col),
        mesh=mesh,
        in_specs=(spec, spec, small, small),
        out_specs=(spec, spec, P()),
        check_vma=False,
    )
```

time: 380 us -> 266 us (0.70)
  Pallas kernels: 0 us -> 217 us
  other arithmetic: 102 us -> 2.12 us
  local copies, waits for them, and re-layouts: 83.1 us -> 5.11 us
  starting transfers between devices: 66.8 us -> 0 us
  waiting for transfers between devices: 47.5 us -> 0 us
  blocking collectives: 69.9 us -> 40.3 us
  matrix products: 7.8 us -> 0 us
    pallas_call x0 -> x4, Pallas kernels: none -> 217 us  [the longest x1 132 us: body(): pl.pallas_call(functools.partial(halo_kernel, n_row, n_col), out_shape=(s...]
    ppermute x16 -> x0, starting transfers between devices: 66.8 us -> none  [the longest x8 55.6 us: with_halo(): before = lax.ppermute(last, axis, up)]
    ppermute x16 -> x0, waiting for transfers between devices: 47.5 us -> none  [the longest x8 33.1 us: with_halo(): after = lax.ppermute(leading, axis, down)]
    concatenate x4 -> x0, other arithmetic: 37.5 us -> none  [with_halo(): value = jnp.concatenate([before, value, after], axis=dim)]
    all_gather x2 -> x0, blocking collectives: 26.8 us -> none  [the longest x1 15.9 us: long_cols(): portion = lax.all_gather(coarse, 'col', axis=2, tiled=True)]
    reduce_sum x4 -> x1, other arithmetic: 26.5 us -> 0.86 us  [body(): totals = lax.psum(jnp.sum(sums, axis=(2, 3)).T, ('row', 'col'))]
    unnamed x18 -> x3, local copies, waits for them, and re-layouts: 24.7 us -> 1.03 us
    gather x12 -> x0, local copies, waits for them, and re-layouts: 21.3 us -> none
  transfers between devices with their start and end apart: 16 -> 0, of which waited for: 9 -> 0; matrix products, arithmetic and copies ran while one was open for 4% -> 0% of each run, Pallas kernels for 0% -> 0%
where the time goes in v1:
time: 266 us; the launch traced here: 265 us
  Pallas kernels  217 us (82%)
  blocking collectives  40.3 us (15%)
  local copies, waits for them, and re-layouts  5.11 us (2%)
    pallas_call x1, Pallas kernels, body(): pl.pallas_call(functools.partial(halo_kernel, n_row, n_col), out_shape=(s...  132 us
    pallas_call x1, Pallas kernels, body(): pl.pallas_call(functools.partial(band_kernel, n_row, n_col), out_shape=(s...  47.7 us
    psum x1, blocking collectives, body(): totals = lax.psum(jnp.sum(sums, axis=(2, 3)).T, ('row', 'col'))  40.3 us
    pallas_call x1, Pallas kernels, body(): pl.pallas_call(shift_kernel, out_shape=(struct((scans, height, length), F...  20.8 us
    pallas_call x1, Pallas kernels, body(): pl.pallas_call(functools.partial(gather_kernel, n_row, n_col), out_shape=...  16.8 us

profile of v1, /device:TPU:0, one launch (start us, length us, event | category | flops | bytes accessed | tf_op | source)
XLA Modules:
  0.0 265.4 jit_solution(10077085702553693438)
XLA Ops:
  0.6 0.6 pad_add_fusion.place
  1.2 1.2 slice.7
  2.4 0.2 copy.20
  2.6 1.1 slice.6
  3.7 0.2 copy.19
  3.9 0.1 pad.1.clone
  4.0 0.7 maximum_bitcast_fusion.extra
  4.7 131.9 %halo.1 = (f32[4,528,1280]{2,1,0:T(8,128)}, f32[6,4,8,256]{3,2,1,0:T(8,128)}) custom-call(f32[4,256,1024]{2,1,0:T(8,128)} %after.1, f32[4,8,256]{2,1,0:T(8,128)} %maximum_bitcast_fusion.extra), custom_call_target="tpu_custom_call" | custom-call | tf_op jit(solution)/shard_map/halo/pallas_call | solution.py:480
  136.6 20.8 %shift.1 = (f32[4,256,1024]{2,1,0:T(8,128)}, f32[4,24,128]{2,1,0:T(8,128)}, f32[4,16,256]{2,1,0:T(8,128)}) custom-call(s32[2]{0:T(128)} %pad_add_fusion.place, s32[2,4]{1,0:T(2,128)} %bitcast.8, s32[2,4]{1,0:T(2,128)} %bitcast.9, f32[4,528,1280]{2,1,0:T(8,128)} %get-tuple-element.15.wide, f32[4,256,1024]{2,1,0:T(8,128)} %before.1, ...), custom_call_target="tpu_custom_call" | custom-call | tf_op jit(solution)/shard_map/shift/pallas_call | solution.py:498
  157.4 1.7 constant_dynamic-slice_fusion.hc
  159.1 16.8 %gather.1 = (f32[2,4,8,1024]{3,2,1,0:T(8,128)}, f32[4,4,8,128]{3,2,1,0:T(8,128)}, f32[2,4,8,256]{3,2,1,0:T(8,128)}, f32[8,4,24,128]{3,2,1,0:T(8,128)}) custom-call(f32[4,256,1024]{2,1,0:T(8,128)} %get-tuple-element.17.diff, f32[4,24,128]{2,1,0:T(8,128)} %get-tuple-element.18.partial, f32[4,16,256]{2,1,0:T(8,128)} %get-tuple-element.19.edges, ...), custom_call_target="tpu_custom_call" | custom-call | tf_op jit(solution)/shard_map/gather/pallas_call | solution.py:527
  175.9 47.7 %band.1 = (f32[4,256,1024]{2,1,0:T(8,128)}, f32[4,256,1024]{2,1,0:T(8,128)}, f32[4,2,8,128]{3,2,1,0:T(8,128)}) custom-call(s32[2]{0:T(128)} %pad_add_fusion.place, f32[4,256,1024]{2,1,0:T(8,128)} %get-tuple-element.17.diff, f32[2,4,8,1024]{3,2,1,0:T(8,128)} %get-tuple-element.20.rows_in, f32[4,4,8,128]{3,2,1,0:T(8,128)} %get-tuple-element.21.corners, ...), custom_call_target="tpu_custom_call" | custom-call | tf_op jit(solution)/shard_map/band/pallas_call | solution.py:549
  223.6 0.9 reduce_sum.9
  224.4 40.3 %psum.7 = f32[2,4]{0,1:T(4,128)S(1)} all-reduce(f32[2,4]{0,1:T(4,128)S(1)} %bitcast.7), channel_id=1, replica_groups=mesh['row'=8,'col'=4] {'row','col'}, use_global_device_ids=true, to_apply=%region_1.2 | all-reduce | flops 8 | bytes 64 | tf_op jit(solution)/shard_map/psum | solution.py:580
  264.7 0.7 copy.18
  (2 shorter events, 0.0 us)

commit v2 on v1

--- a/solution.py
+++ b/solution.py
@@ -3,6 +3,7 @@
 
 import jax
 import jax.numpy as jnp
+import ml_dtypes
 import numpy as np
 from jax import lax
 from jax.experimental import pallas as pl
@@ -96,6 +97,12 @@
     return table
 
 
+def halves(table):
+    high = table.astype(ml_dtypes.bfloat16)
+    low = (table - high.astype(np.float64)).astype(ml_dtypes.bfloat16)
+    return np.concatenate([high, low], axis=1)
+
+
 @functools.lru_cache(maxsize=None)
 def tables(nr, nc, tr, tc):
     n_row, n_col = nr // tr, nc // tc
@@ -110,7 +117,7 @@
         for b in range(-1, bc + 1):
             target = part * bc + b
             if 0 <= target < nc // BLOCK:
-                hc[part, :, :, b + 1] = col_spread[target]
+                hc[:, part, :, b + 1] = col_spread[target]
         up = upsample_rows(nc, part * tc - LANES, tc + 2 * LANES)
         for b in range(-1, bc + 1):
             target = part * bc + b
@@ -134,7 +141,18 @@
             q = part * tc - LANES + n
             if 0 <= q < nc:
                 cw[part, 0, n] = 1.0 / col_weight[q]
-    return [t.astype(np.float32) for t in (r_table, c_table, hc, cu, ru, rw, cw)]
+    gc = np.zeros((4 * LANES, 2 * LANES))
+    for n in range(2 * LANES):
+        for k in range(-SR, SR + 1):
+            gc[n + LANES + k, n] = TAPS[k + SR]
+    tall = tr + 2 * EDGE
+    gr = np.zeros((n_row, tall, tall))
+    for part in range(n_row):
+        for n in range(SR, tall - SR):
+            for k in range(-SR, SR + 1):
+                gr[part, n, n + k] = TAPS[k + SR] * rw[part, n, 0]
+    wide = [t.astype(np.float32) for t in (c_table, hc, cu, ru, cw)]
+    return wide + [halves(t) for t in (r_table, gc[None], gr)]
 
 
 def remote(src, dst, send, recv, device):
@@ -161,7 +179,7 @@
     return found
 
 
-def halo_kernel(n_row, n_col, after, extra, wide, slots, own_sem, send, recv, slot_send, slot_recv):
+def halo_kernel(n_row, n_col, after, extra, ends, flanks, slots, send, recv, slot_send, slot_recv):
     scans, height, length = after.shape
     near = neighbours(n_row, n_col)
     barrier = pltpu.get_barrier_semaphore()
@@ -174,27 +192,25 @@
             signal(barrier, device)
 
     pl.semaphore_wait(barrier, count)
-    low, high = HALO, HALO + height
-    bands = {-1: (0, HALO), 0: (low, height), 1: (high, HALO)}
-    mid = pl.ds(LANES, length)
 
     def row_copy(s, dr):
         src = pl.ds(height - HALO, HALO) if dr == 1 else pl.ds(0, HALO)
-        dst = pl.ds(0, HALO) if dr == 1 else pl.ds(high, HALO)
         k = 0 if dr == 1 else 1
         return remote(
-            after.at[s, src, :], wide.at[s, dst, mid], send.at[k, s], recv.at[k, s], near[dr, 0][1]
+            after.at[s, src, :], ends.at[k, s, :, pl.ds(LANES, length)],
+            send.at[k, s], recv.at[k, s], near[dr, 0][1],
         )
 
     def col_copy(s, dc, band):
-        start, rows = bands[band]
-        k = 2 + (band + 1) * 2 + (0 if dc == 1 else 1)
+        side = 0 if dc == 1 else 1
+        k = 2 + (band + 1) * 2 + side
         first = length - LANES if dc == 1 else 0
         if band == 0:
-            src = after.at[s, :, pl.ds(first, LANES)]
+            src, dst = after.at[s, :, pl.ds(first, LANES)], flanks.at[side, s]
         else:
-            src = wide.at[s, pl.ds(start, rows), pl.ds(LANES + first, LANES)]
-        dst = wide.at[s, pl.ds(start, rows), pl.ds(0 if dc == 1 else LANES + length, LANES)]
+            v = 0 if band == -1 else 1
+            src = ends.at[v, s, :, pl.ds(LANES + first, LANES)]
+            dst = ends.at[v, s, :, pl.ds(0 if dc == 1 else LANES + length, LANES)]
         return remote(src, dst, send.at[k, s], recv.at[k, s], near[0, dc][1])
 
     def slot_copy(dr, dc):
@@ -210,8 +226,6 @@
     for s in range(scans):
         for dc in (1, -1):
             when(near[0, dc][0], col_copy(s, dc, 0).start)
-    own = pltpu.make_async_copy(after, wide.at[:, pl.ds(low, height), mid], own_sem)
-    own.start()
     for dc in (1, -1):
         for dr in (-1, 0, 1):
             when(near[dr, dc][0], slot_copy(dr, dc).start)
@@ -233,7 +247,11 @@
         for dr in (-1, 0, 1):
             when(near[dr, dc][0], slot_copy(dr, dc).wait_send)
             when(near[-dr, -dc][0], slot_copy(dr, dc).wait_recv)
-    own.wait()
+
+
+def split2(value):
+    high = value.astype(BF16)
+    return high, (value - high.astype(F32)).astype(BF16)
 
 
 def split3(value):
@@ -255,7 +273,8 @@
     )
 
 
-def shift_kernel(place, offsets, fractions, wide, before, slots, r_tab, c_tab, diff, partial, edges, tail):
+def shift_kernel(place, offsets, fractions, after, ends, flanks, before, slots, r_tab, c_tab, h_tab,
+                 diff, partial, edges, wide):
     s = pl.program_id(0)
     height, length = before.shape[1], before.shape[2]
     total = length + 3 * LANES
@@ -263,15 +282,21 @@
     rt = cubic(fractions[0, s].astype(F32) / 256.0)
     ct = cubic(fractions[1, s].astype(F32) / 256.0)
     blank = jnp.zeros((LANES - 16, height), F32)
+    spare = slice(length + 2 * LANES, total)
     for j in range(3):
         block = jnp.concatenate([slots[3 + j, 0], blank, slots[j, 0]], axis=0)
         flipped = jnp.transpose(block)
         if j == 0:
-            tail[0:HALO] = flipped[height - HALO :]
+            wide[0:HALO, spare] = flipped[height - HALO :]
         elif j == 1:
-            tail[HALO : HALO + height] = flipped
+            wide[HALO : HALO + height, spare] = flipped
         else:
-            tail[HALO + height :] = flipped[:HALO]
+            wide[HALO + height :, spare] = flipped[:HALO]
+    wide[0:HALO, 0 : length + 2 * LANES] = ends[0, 0]
+    wide[HALO : HALO + height, 0:LANES] = flanks[0, 0]
+    wide[HALO : HALO + height, LANES : LANES + length] = after[0]
+    wide[HALO : HALO + height, LANES + length : length + 2 * LANES] = flanks[1, 0]
+    wide[HALO + height :, 0 : length + 2 * LANES] = ends[1, 0]
     turn = 2 * total - LANES - dc + 1
     turn = lax.rem(turn, total)
     start = HALO - 1 + dr
@@ -281,9 +306,7 @@
         first = start + r * rows
         base = pl.multiple_of((first // 8) * 8, 8)
         off = first - base
-        x = jnp.concatenate(
-            [wide[0, pl.ds(base, rows + 16), :], tail[pl.ds(base, rows + 16), :]], axis=1
-        )
+        x = wide[pl.ds(base, rows + 16), :]
         x = pltpu.roll(x, lax.rem(rows + 16 - off, rows + 16), 0)
         y = rt[0] * x[0:rows] + rt[1] * x[1 : rows + 1] + rt[2] * x[2 : rows + 2] + rt[3] * x[3 : rows + 3]
         y = pltpu.roll(y, turn, 1)
@@ -295,14 +318,19 @@
         return carry
 
     lax.fori_loop(0, height // rows, step, 0)
-    d = diff[0]
-    mixed = jnp.dot(r_tab[0], d, precision=HIGHEST, preferred_element_type=F32)
-    partial[0] = jnp.dot(mixed, c_tab[0], precision=HIGHEST, preferred_element_type=F32)
+    high, low = split2(diff[0])
+    rr = r_tab[0]
+    pr = rr.shape[0] // 2
+    both = jnp.dot(rr, high, preferred_element_type=F32)
+    mixed = both[:pr] + both[pr:] + jnp.dot(rr[:pr], low, preferred_element_type=F32)
+    here = jnp.dot(mixed, c_tab[0], precision=HIGHEST, preferred_element_type=F32)
+    for t in range(partial.shape[0]):
+        partial[t, 0] = jnp.dot(here, h_tab[0, t], precision=HIGHEST, preferred_element_type=F32)
     edges[0, 0:EDGE] = jnp.transpose(diff[0, :, 0:LANES])[0:EDGE]
     edges[0, EDGE:] = jnp.transpose(diff[0, :, length - LANES :])[LANES - EDGE :]
 
 
-def gather_kernel(n_row, n_col, diff, partial, edges, hc, rows_out, corners, sides, spread, parts,
+def gather_kernel(n_row, n_col, diff, partial, edges, rows_out, corners, sides, spread, parts,
                   psend, precv, qsend, qrecv, nsend, nrecv):
     scans, height, length = diff.shape
     near = neighbours(n_row, n_col)
@@ -324,8 +352,9 @@
     pl.semaphore_wait(barrier, count)
 
     def p_copy(k):
+        target = lax.rem(col + k, n_col)
         return remote(
-            partial, parts.at[col], psend.at[k - 1], precv.at[k - 1], (row, lax.rem(col + k, n_col))
+            partial.at[target], parts.at[col], psend.at[k - 1], precv.at[k - 1], (row, target)
         )
 
     def q_copy(k):
@@ -354,19 +383,11 @@
         p_copy(k).start()
     for (dr, dc), (exists, _) in near.items():
         pl.when(exists)(near_copy(dr, dc).start)
-    own = [
-        jnp.dot(partial[s], hc[0, col], precision=HIGHEST, preferred_element_type=F32)
-        for s in range(scans)
-    ]
+    own = partial[col]
     for k in range(1, n_col):
         p_copy(k).wait_recv()
-        source = lax.rem(col - k + n_col, n_col)
-        for s in range(scans):
-            own[s] = own[s] + jnp.dot(
-                parts[source, s], hc[0, source], precision=HIGHEST, preferred_element_type=F32
-            )
-    for s in range(scans):
-        spread[row, s] = own[s]
+        own = own + parts[lax.rem(col - k + n_col, n_col)]
+    spread[row] = own
     for k in range(1, n_row):
         q_copy(k).start()
     for k in range(1, n_col):
@@ -379,8 +400,8 @@
         q_copy(k).wait_recv()
 
 
-def band_kernel(n_row, n_col, place, diff, rows_in, corners, sides, spread, ru, cu, rw, cw,
-                band_out, slope_out, sums, x, a, b):
+def band_kernel(n_row, n_col, place, diff, rows_in, corners, sides, spread, ru, cu, cw, gc, gr,
+                band_out, slope_out, sums, x, b):
     row, col = place[0], place[1]
     height, length = diff.shape[1], diff.shape[2]
     width = length + 2 * LANES
@@ -404,41 +425,28 @@
         jnp.concatenate([right, blank], axis=0)
     )
 
-    def across(r, carry):
-        here = pl.ds(pl.multiple_of(r * 16, 16), 16)
-        v = x[here, :]
-        total = TAPS[SR] * v
-        for k in range(1, SR + 1):
-            total = total + TAPS[SR + k] * (pltpu.roll(v, k, 1) + pltpu.roll(v, width - k, 1))
-        a[here, :] = total * cw[0]
-        return carry
-
-    lax.fori_loop(0, tall // 16, across, 0)
+    high, low = split2(x[...])
+    both = jnp.concatenate([high, low], axis=0)
+    pieces = []
+    for first in range(0, width, 2 * LANES):
+        begin, end = max(first - LANES, 0), min(first + 3 * LANES, width)
+        skip = begin - (first - LANES)
+        g_high = gc[0, skip : skip + end - begin, :]
+        g_low = gc[0, 4 * LANES + skip : 4 * LANES + skip + end - begin, :]
+        two = jnp.dot(both[:, begin:end], g_high, preferred_element_type=F32)
+        pieces.append(
+            two[:tall] + two[tall:]
+            + jnp.dot(high[:, begin:end], g_low, preferred_element_type=F32)
+        )
+    high, low = split2(jnp.concatenate(pieces, axis=1) * cw[0])
+    two = jnp.dot(gr[0], high, preferred_element_type=F32)
+    smooth = two[:tall] + two[tall:] + jnp.dot(gr[0, :tall], low, preferred_element_type=F32)
     q = jnp.concatenate([spread[i, 0] for i in range(n_row)], axis=0)
     mixed = jnp.dot(ru[0], q, precision=HIGHEST, preferred_element_type=F32)
     pieces = jnp.concatenate(split3(mixed), axis=1)
     cub = cu[0].astype(BF16)
     wavy = jnp.dot(pieces, jnp.concatenate([cub, cub, cub], axis=0), preferred_element_type=F32)
-    b[...] = wavy
-
-    def along(r, carry):
-        base = pl.multiple_of(r * 8, 8)
-        v = a[pl.ds(base, 24), :]
-        total = TAPS[SR] * v[8:16]
-        for k in range(1, SR + 1):
-            total = total + TAPS[SR + k] * (v[8 - k : 16 - k] + v[8 + k : 16 + k])
-        here = pl.ds(base + 8, 8)
-        b[here, :] = total * rw[0, here, :] - b[here, :]
-        return carry
-
-    lax.fori_loop(0, height // 8, along, 0)
-    for edge in (EDGE - 1, EDGE + height):
-        total = TAPS[SR] * a[edge : edge + 1, :]
-        for k in range(1, SR + 1):
-            total = total + TAPS[SR + k] * (
-                a[edge - k : edge - k + 1, :] + a[edge + k : edge + k + 1, :]
-            )
-        b[edge : edge + 1, :] = total * rw[0, edge : edge + 1, :] - b[edge : edge + 1, :]
+    b[...] = smooth - wavy
 
     lane = lax.broadcasted_iota(jnp.int32, (1, length), 1) + col * length
     col_mask = ((lane >= 1) & (lane <= n_col * length - 2)).astype(F32)
@@ -459,17 +467,68 @@
         return carry[0] + field * field, carry[1] + value
 
     start = jnp.zeros((8, length), F32)
-    heights, slopes = lax.fori_loop(0, height // 8, slope, (start, start))
+    heights, slopes = lax.fori_loop(0, height // 8, slope, (start, start), unroll=2)
     sums[0, 0] = sum(heights[:, i : i + LANES] for i in range(0, length, LANES))
     sums[0, 1] = sum(slopes[:, i : i + LANES] for i in range(0, length, LANES))
+
+
+def total_kernel(n_row, n_col, cells, sums, out, held, parts, psend, precv, qsend, qrecv):
+    row, col = lax.axis_index("row"), lax.axis_index("col")
+    scans = sums.shape[0]
+    barrier = pltpu.get_barrier_semaphore()
+    for k in range(1, n_col):
+        signal(barrier, (row, lax.rem(col + k, n_col)))
+    for k in range(1, n_row):
+        signal(barrier, (lax.rem(row + k, n_row), col))
+    for k in range(2):
+        for s in range(scans):
+            held[0, k * scans + s : k * scans + s + 1] = jnp.sum(sums[s, k], axis=0, keepdims=True)
+    pl.semaphore_wait(barrier, n_row + n_col - 2)
+
+    def p_copy(k):
+        return remote(
+            held.at[0], parts.at[k - 1], psend.at[k - 1], precv.at[k - 1],
+            (row, lax.rem(col + k, n_col)),
+        )
+
+    def q_copy(k):
+        slot = n_col - 1 + k - 1
+        return remote(
+            held.at[1], parts.at[slot], qsend.at[k - 1], qrecv.at[k - 1],
+            (lax.rem(row + k, n_row), col),
+        )
+
+    for k in range(1, n_col):
+        p_copy(k).start()
+    value = held[0]
+    for k in range(1, n_col):
+        p_copy(k).wait_recv()
+        value = value + parts[k - 1]
+    held[1] = value
+    for k in range(1, n_row):
+        q_copy(k).start()
+    for k in range(1, n_row):
+        q_copy(k).wait_recv()
+        value = value + parts[n_col - 1 + k - 1]
+    result = jnp.sqrt(jnp.sum(value, axis=1, keepdims=True) / cells + EPSILON)
+    spread = jnp.broadcast_to(result, value.shape)
+    index = lax.broadcasted_iota(jnp.int32, value.shape, 0)
+    lane = lax.broadcasted_iota(jnp.int32, value.shape, 1)
+    for k in range(2):
+        picked = jnp.sum(jnp.where(index == k * scans + lane, spread, 0.0), axis=0, keepdims=True)
+        out[k : k + 1, :] = picked[:, 0:scans]
+    for k in range(1, n_col):
+        p_copy(k).wait_send()
+    for k in range(1, n_row):
+        q_copy(k).wait_send()
 
 
 def body(n_row, n_col, before, after, offsets, fractions):
     scans, height, length = before.shape
     width = length + 2 * LANES
     tall = height + 2 * EDGE
-    r_tab, c_tab, hc, cu, ru, rw, cw = tables(n_row * height, n_col * length, height, length)
-    pr = r_tab.shape[1]
+    c_tab, hc, cu, ru, cw, r_tab, gc, gr = tables(n_row * height, n_col * length, height, length)
+    pr = r_tab.shape[1] // 2
     place = jnp.stack([lax.axis_index("row"), lax.axis_index("col")]).astype(jnp.int32)
     filler = jnp.zeros((scans, height, 5), F32)
     extra = jnp.concatenate(
@@ -477,21 +536,23 @@
     ).transpose(0, 2, 1)
     struct = jax.ShapeDtypeStruct
     dma = pltpu.SemaphoreType.DMA
-    wide, slots = pl.pallas_call(
+    ends, flanks, slots = pl.pallas_call(
         functools.partial(halo_kernel, n_row, n_col),
         out_shape=(
-            struct((scans, height + 2 * HALO, width), F32),
+            struct((2, scans, HALO, width), F32),
+            struct((2, scans, height, LANES), F32),
             struct((6, scans, 8, height), F32),
         ),
         in_specs=[ANY, ANY],
-        out_specs=(ANY, ANY),
-        scratch_shapes=[dma, dma((8, scans)), dma((8, scans)), dma((6,)), dma((6,))],
+        out_specs=(ANY, ANY, ANY),
+        scratch_shapes=[dma((8, scans)), dma((8, scans)), dma((6,)), dma((6,))],
         compiler_params=pltpu.CompilerParams(
             collective_id=0, has_side_effects=True, vmem_limit_bytes=VMEM_LIMIT
         ),
         name="halo",
     )(after, extra)
 
+    all_scan = lambda s, *_: (0, s, 0, 0)
     by_scan = lambda s, *_: (s, 0, 0)
     row_part = lambda s, p, *_: (p[0], 0, 0)
     col_part = lambda s, p, *_: (p[1], 0, 0)
@@ -499,31 +560,33 @@
         shift_kernel,
         out_shape=(
             struct((scans, height, length), F32),
-            struct((scans, pr, LANES), F32),
+            struct((n_col, scans, pr, LANES), F32),
             struct((scans, 2 * EDGE, height), F32),
         ),
         grid_spec=pltpu.PrefetchScalarGridSpec(
             num_scalar_prefetch=3,
             grid=(scans,),
             in_specs=[
-                pl.BlockSpec((1, height + 2 * HALO, width), by_scan),
+                pl.BlockSpec((1, height, length), by_scan),
+                pl.BlockSpec((2, 1, HALO, width), all_scan),
+                pl.BlockSpec((2, 1, height, LANES), all_scan),
                 pl.BlockSpec((1, height, length), by_scan),
                 pl.BlockSpec((6, 1, 8, height), lambda s, *_: (0, s, 0, 0)),
-                pl.BlockSpec((1, pr, height), row_part),
+                pl.BlockSpec((1, 2 * pr, height), row_part),
                 pl.BlockSpec((1, length, LANES), col_part),
+                pl.BlockSpec((1, n_col, LANES, LANES), lambda s, p, *_: (p[1], 0, 0, 0)),
             ],
             out_specs=(
                 pl.BlockSpec((1, height, length), by_scan),
-                pl.BlockSpec((1, pr, LANES), by_scan),
+                pl.BlockSpec((n_col, 1, pr, LANES), all_scan),
                 pl.BlockSpec((1, 2 * EDGE, height), by_scan),
             ),
-            scratch_shapes=[pltpu.VMEM((height + 2 * HALO, LANES), F32)],
+            scratch_shapes=[pltpu.VMEM((height + 2 * HALO, width + LANES), F32)],
         ),
         compiler_params=pltpu.CompilerParams(vmem_limit_bytes=VMEM_LIMIT),
         name="shift",
-    )(place, offsets[:, :, 0, 0], fractions[:, :, 0, 0], wide, before, slots, r_tab, c_tab)
-
-    hc_here = lax.dynamic_index_in_dim(jnp.asarray(hc), place[1], 0, keepdims=True)
+    )(place, offsets[:, :, 0, 0], fractions[:, :, 0, 0], after, ends, flanks, before, slots, r_tab, c_tab, hc)
+
     rows_out, corners, sides, spread = pl.pallas_call(
         functools.partial(gather_kernel, n_row, n_col),
         out_shape=(
@@ -532,7 +595,7 @@
             struct((2, scans, EDGE, height), F32),
             struct((n_row, scans, pr, LANES), F32),
         ),
-        in_specs=[ANY, VM, VM, VM],
+        in_specs=[ANY, VM, VM],
         out_specs=(VM, VM, VM, VM),
         scratch_shapes=[
             pltpu.VMEM((n_col, scans, pr, LANES), F32),
@@ -543,9 +606,8 @@
             collective_id=1, has_side_effects=True, vmem_limit_bytes=VMEM_LIMIT
         ),
         name="gather",
-    )(diff, partial, edges, hc_here)
-
-    all_scan = lambda s, *_: (0, s, 0, 0)
+    )(diff, partial, edges)
+
     band, slope, sums = pl.pallas_call(
         functools.partial(band_kernel, n_row, n_col),
         out_shape=(
@@ -564,22 +626,34 @@
                 pl.BlockSpec((n_row, 1, pr, LANES), all_scan),
                 pl.BlockSpec((1, tall, n_row * pr), row_part),
                 pl.BlockSpec((1, LANES, width), col_part),
-                pl.BlockSpec((1, tall, 1), row_part),
                 pl.BlockSpec((1, 1, width), col_part),
+                pl.BlockSpec((1, 8 * LANES, 2 * LANES), lambda s, *_: (0, 0, 0)),
+                pl.BlockSpec((1, 2 * tall, tall), row_part),
             ],
             out_specs=(
                 pl.BlockSpec((1, height, length), by_scan),
                 pl.BlockSpec((1, height, length), by_scan),
                 pl.BlockSpec((1, 2, 8, LANES), lambda s, *_: (s, 0, 0, 0)),
             ),
-            scratch_shapes=[pltpu.VMEM((tall, width), F32)] * 3,
+            scratch_shapes=[pltpu.VMEM((tall, width), F32)] * 2,
         ),
         compiler_params=pltpu.CompilerParams(vmem_limit_bytes=VMEM_LIMIT),
         name="band",
-    )(place, diff, rows_out, corners, sides, spread, ru, cu, rw, cw)
-    totals = lax.psum(jnp.sum(sums, axis=(2, 3)).T, ("row", "col"))
-    cells = n_row * height * n_col * length
-    return band, slope, jnp.sqrt(totals / cells + EPSILON)
+    )(place, diff, rows_out, corners, sides, spread, ru, cu, cw, gc, gr)
+    params = pl.pallas_call(
+        functools.partial(total_kernel, n_row, n_col, float(n_row * height * n_col * length)),
+        out_shape=struct((2, scans), F32),
+        in_specs=[VM],
+        out_specs=VM,
+        scratch_shapes=[
+            pltpu.VMEM((2, 2 * scans, LANES), F32),
+            pltpu.VMEM((n_row + n_col - 2, 2 * scans, LANES), F32),
+            dma((n_col - 1,)), dma((n_col - 1,)), dma((n_row - 1,)), dma((n_row - 1,)),
+        ],
+        compiler_params=pltpu.CompilerParams(collective_id=2, has_side_effects=True),
+        name="total",
+    )(sums)
+    return band, slope, params
 
 
 def solution(mesh):

time: 266 us -> 140 us (0.53)
  Pallas kernels: 217 us -> 134 us
  blocking collectives: 40.3 us -> 0 us
    pallas_call x1, Pallas kernels: 132 us -> 25.4 us  [body(): pl.pallas_call(functools.partial(halo_kernel, n_row, n_col), out_shape=(s...]
    psum x1 -> x0, blocking collectives: 40.3 us -> none  [body(): totals = lax.psum(jnp.sum(sums, axis=(2, 3)).T, ('row', 'col'))]
    pallas_call x1, Pallas kernels: 16.8 us -> 51.5 us  [body(): pl.pallas_call(functools.partial(gather_kernel, n_row, n_col), out_shape=...]
    pallas_call x1, Pallas kernels: 47.7 us -> 25.2 us  [body(): pl.pallas_call(functools.partial(band_kernel, n_row, n_col), out_shape=(s...]
    pallas_call x0 -> x1, Pallas kernels: none -> 10.4 us  [body(): pl.pallas_call(functools.partial(total_kernel, n_row, n_col, float(n_row...]
where the time goes in v2:
time: 140 us
  Pallas kernels  134 us (96%)
  local copies, waits for them, and re-layouts  3.98 us (3%)
    pallas_call x1, Pallas kernels, body(): pl.pallas_call(functools.partial(gather_kernel, n_row, n_col), out_shape=...  51.5 us
    pallas_call x1, Pallas kernels, body(): pl.pallas_call(functools.partial(halo_kernel, n_row, n_col), out_shape=(s...  25.4 us
    pallas_call x1, Pallas kernels, body(): pl.pallas_call(functools.partial(band_kernel, n_row, n_col), out_shape=(s...  25.2 us
    pallas_call x1, Pallas kernels, body(): pl.pallas_call(shift_kernel, out_shape=(struct((scans, height, length), F...  21.6 us
    pallas_call x1, Pallas kernels, body(): pl.pallas_call(functools.partial(total_kernel, n_row, n_col, float(n_row...  10.4 us

profile of v2, /device:TPU:0, one launch (start us, length us, event | category | flops | bytes accessed | tf_op | source)
XLA Modules:
  0.0 140.1 jit_solution(5333284496103831278)
XLA Ops:
  0.6 0.6 pad_add_fusion.place
  1.2 0.1 pad.1.clone
  1.3 1.1 slice.6
  2.4 0.2 copy.17
  2.6 1.3 slice.7
  3.8 0.2 copy.18
  4.0 0.7 maximum_bitcast_fusion.extra
  4.7 25.4 %halo.1 = (f32[2,4,136,1280]{3,2,1,0:T(8,128)}, f32[2,4,256,128]{3,2,1,0:T(8,128)}, f32[6,4,8,256]{3,2,1,0:T(8,128)}) custom-call(f32[4,256,1024]{2,1,0:T(8,128)} %after.3, f32[4,8,256]{2,1,0:T(8,128)} %maximum_bitcast_fusion.extra), custom_call_target="tpu_custom_call" | custom-call | tf_op jit(solution)/shard_map/halo/pallas_call | solution.py:539
  30.1 21.6 %shift.1 = (f32[4,256,1024]{2,1,0:T(8,128)}, f32[4,4,24,128]{3,2,1,0:T(8,128)}, f32[4,16,256]{2,1,0:T(8,128)}) custom-call(s32[2]{0:T(128)} %pad_add_fusion.place, s32[2,4]{1,0:T(2,128)} %bitcast.6, s32[2,4]{1,0:T(2,128)} %bitcast.7, f32[4,256,1024]{2,1,0:T(8,128)} %after.3, f32[2,4,136,1280]{3,2,1,0:T(8,128)} %get-tuple-element.16.ends, ...), custom_call_target="tpu_custom_call" | custom-call | tf_op jit(solution)/shard_map/shift/pallas_call | solution.py:559
  51.7 51.5 %gather.1 = (f32[2,4,8,1024]{3,2,1,0:T(8,128)}, f32[4,4,8,128]{3,2,1,0:T(8,128)}, f32[2,4,8,256]{3,2,1,0:T(8,128)}, f32[8,4,24,128]{3,2,1,0:T(8,128)}) custom-call(f32[4,256,1024]{2,1,0:T(8,128)} %get-tuple-element.19.diff, f32[4,4,24,128]{3,2,1,0:T(8,128)} %get-tuple-element.20.partial, f32[4,16,256]{2,1,0:T(8,128)} %get-tuple-element.21.edges), custom_call_target="tpu_custom_call" | custom-call | tf_op jit(solution)/shard_map/gather/pallas_call | solution.py:590
  103.3 25.2 %band.1 = (f32[4,256,1024]{2,1,0:T(8,128)}, f32[4,256,1024]{2,1,0:T(8,128)}, f32[4,2,8,128]{3,2,1,0:T(8,128)}) custom-call(s32[2]{0:T(128)} %pad_add_fusion.place, f32[4,256,1024]{2,1,0:T(8,128)} %get-tuple-element.19.diff, f32[2,4,8,1024]{3,2,1,0:T(8,128)} %get-tuple-element.22.rows_in, f32[4,4,8,128]{3,2,1,0:T(8,128)} %get-tuple-element.23.corners, ...), custom_call_target="tpu_custom_call" | custom-call | tf_op jit(solution)/shard_map/band/pallas_call | solution.py:611
  128.5 10.4 %total.1 = f32[2,4]{1,0:T(2,128)} custom-call(f32[4,2,8,128]{3,2,1,0:T(8,128)} %get-tuple-element.28.sums), custom_call_target="tpu_custom_call" | custom-call | tf_op jit(solution)/shard_map/total/pallas_call | solution.py:643
  138.9 1.2 copy.20
  (1 shorter events, 0.0 us)

commit v3 on v2

--- a/solution.py
+++ b/solution.py
@@ -179,7 +179,8 @@
     return found
 
 
-def halo_kernel(n_row, n_col, after, extra, ends, flanks, slots, send, recv, slot_send, slot_recv):
+def halo_kernel(n_row, n_col, after, extra, ends, flanks, slots, via, send, recv, slot_send, slot_recv,
+                via_send, via_recv):
     scans, height, length = after.shape
     near = neighbours(n_row, n_col)
     barrier = pltpu.get_barrier_semaphore()
@@ -191,6 +192,18 @@
         def _():
             signal(barrier, device)
 
+    row, col = lax.axis_index("row"), lax.axis_index("col")
+    relayed = range(scans // 2, scans) if n_row == 8 else range(0)
+    routes = {1: (3, 7, 4), -1: (4, 0, 3)}
+    if relayed:
+        for one, others in ((0, (3, 4)), (7, (3, 4)), (3, (0, 7)), (4, (0, 7))):
+            count += jnp.where(row == one, 2, 0)
+
+            @pl.when(row == one)
+            def _():
+                for other in others:
+                    signal(barrier, (other, col))
+
     pl.semaphore_wait(barrier, count)
 
     def row_copy(s, dr):
@@ -199,6 +212,21 @@
         return remote(
             after.at[s, src, :], ends.at[k, s, :, pl.ds(LANES, length)],
             send.at[k, s], recv.at[k, s], near[dr, 0][1],
+        )
+
+    def first_leg(s, dr):
+        src = pl.ds(height - HALO, HALO) if dr == 1 else pl.ds(0, HALO)
+        k = 0 if dr == 1 else 1
+        return remote(
+            after.at[s, src, :], via.at[s - relayed[0]],
+            send.at[k, s], via_recv.at[s - relayed[0]], (routes[dr][1], col),
+        )
+
+    def second_leg(s, dr):
+        k = 0 if dr == 1 else 1
+        return remote(
+            via.at[s - relayed[0]], ends.at[k, s, :, pl.ds(LANES, length)],
+            via_send.at[s - relayed[0]], recv.at[k, s], (routes[dr][2], col),
         )
 
     def col_copy(s, dc, band):
@@ -220,15 +248,25 @@
     def when(pred, action):
         pl.when(pred)(action)
 
+    for s in relayed:
+        for dr in (1, -1):
+            when(row == routes[dr][0], first_leg(s, dr).start)
     for s in range(scans):
         for dr in (1, -1):
-            when(near[dr, 0][0], row_copy(s, dr).start)
+            direct = near[dr, 0][0]
+            if s in relayed:
+                direct = direct & (row != routes[dr][0])
+            when(direct, row_copy(s, dr).start)
     for s in range(scans):
         for dc in (1, -1):
             when(near[0, dc][0], col_copy(s, dc, 0).start)
     for dc in (1, -1):
         for dr in (-1, 0, 1):
             when(near[dr, dc][0], slot_copy(dr, dc).start)
+    for s in relayed:
+        for dr in (1, -1):
+            when(row == routes[dr][1], first_leg(s, dr).wait_recv)
+            when(row == routes[dr][1], second_leg(s, dr).start)
     for s in range(scans):
         for dr in (1, -1):
             source = near[-dr, 0][0]
@@ -243,6 +281,9 @@
                 ok = jnp.bool_(True) if band == 0 else near[band, 0][0]
                 when(ok & near[0, dc][0], col_copy(s, dc, band).wait_send)
                 when(ok & near[0, -dc][0], col_copy(s, dc, band).wait_recv)
+    for s in relayed:
+        for dr in (1, -1):
+            when(row == routes[dr][1], second_leg(s, dr).wait_send)
     for dc in (1, -1):
         for dr in (-1, 0, 1):
             when(near[dr, dc][0], slot_copy(dr, dc).wait_send)
@@ -273,51 +314,72 @@
     )
 
 
-def shift_kernel(place, offsets, fractions, after, ends, flanks, before, slots, r_tab, c_tab, h_tab,
-                 diff, partial, edges, wide):
+def shift_kernel(n_col, place, offsets, fractions, after, ends, flanks, before, slots, r_tab, c_tab,
+                 h_tab, diff, partial, edges, wide, mid):
     s = pl.program_id(0)
     height, length = before.shape[1], before.shape[2]
-    total = length + 3 * LANES
-    dr, dc = offsets[0, s], offsets[1, s]
-    rt = cubic(fractions[0, s].astype(F32) / 256.0)
-    ct = cubic(fractions[1, s].astype(F32) / 256.0)
-    blank = jnp.zeros((LANES - 16, height), F32)
-    spare = slice(length + 2 * LANES, total)
-    for j in range(3):
-        block = jnp.concatenate([slots[3 + j, 0], blank, slots[j, 0]], axis=0)
-        flipped = jnp.transpose(block)
-        if j == 0:
-            wide[0:HALO, spare] = flipped[height - HALO :]
-        elif j == 1:
-            wide[HALO : HALO + height, spare] = flipped
-        else:
-            wide[HALO + height :, spare] = flipped[:HALO]
-    wide[0:HALO, 0 : length + 2 * LANES] = ends[0, 0]
-    wide[HALO : HALO + height, 0:LANES] = flanks[0, 0]
-    wide[HALO : HALO + height, LANES : LANES + length] = after[0]
-    wide[HALO : HALO + height, LANES + length : length + 2 * LANES] = flanks[1, 0]
-    wide[HALO + height :, 0 : length + 2 * LANES] = ends[1, 0]
-    turn = 2 * total - LANES - dc + 1
-    turn = lax.rem(turn, total)
+    width = length + 2 * LANES
+    dr, dc = offsets[0, s, 0, 0], offsets[1, s, 0, 0]
+    rt = cubic(fractions[0, s, 0, 0].astype(F32) / 256.0)
+    ct = cubic(fractions[1, s, 0, 0].astype(F32) / 256.0)
+    zero = jnp.float32(0.0)
+    has_left, has_right = place[1] > 0, place[1] < n_col - 1
+    first, last = slice(0, LANES), slice(length + 3 * LANES, length + 4 * LANES)
+    left, inner = slice(LANES, 2 * LANES), slice(2 * LANES, 2 * LANES + length)
+    right = slice(2 * LANES + length, 3 * LANES + length)
+    blank = jnp.zeros((LANES - 8, height), F32)
+    spans = (
+        (slice(0, HALO), slice(height - HALO, height)),
+        (slice(HALO, HALO + height), slice(0, height)),
+        (slice(HALO + height, height + 2 * HALO), slice(0, HALO)),
+    )
+    for j, (here, part) in enumerate(spans):
+        low = jnp.transpose(jnp.concatenate([blank, slots[j, 0]], axis=0))
+        high = jnp.transpose(jnp.concatenate([slots[3 + j, 0], blank], axis=0))
+        wide[here, first] = jnp.where(has_left, low[part], zero)
+        wide[here, last] = jnp.where(has_right, high[part], zero)
+    for v in range(2):
+        here = spans[2 * v][0]
+        wide[here, left] = jnp.where(has_left, ends[v, 0, :, 0:LANES], zero)
+        wide[here, inner] = ends[v, 0, :, LANES : LANES + length]
+        wide[here, right] = jnp.where(has_right, ends[v, 0, :, LANES + length :], zero)
+    here = spans[1][0]
+    wide[here, left] = jnp.where(has_left, flanks[0, 0], zero)
+    wide[here, inner] = after[0]
+    wide[here, right] = jnp.where(has_right, flanks[1, 0], zero)
     start = HALO - 1 + dr
+    lane = 2 * LANES - 1 + dc
+    lane_base = pl.multiple_of((lane // LANES) * LANES, LANES)
+    turn = lane - lane_base
     rows = 32
 
     def step(r, carry):
-        first = start + r * rows
-        base = pl.multiple_of((first // 8) * 8, 8)
-        off = first - base
-        x = wide[pl.ds(base, rows + 16), :]
+        top = start + r * rows
+        base = pl.multiple_of((top // 8) * 8, 8)
+        off = top - base
+        x = wide[pl.ds(base, rows + 16), pl.ds(lane_base, width)]
         x = pltpu.roll(x, lax.rem(rows + 16 - off, rows + 16), 0)
         y = rt[0] * x[0:rows] + rt[1] * x[1 : rows + 1] + rt[2] * x[2 : rows + 2] + rt[3] * x[3 : rows + 3]
-        y = pltpu.roll(y, turn, 1)
-        z = ct[0] * y[:, 0:length]
-        for b in range(1, 4):
-            z = z + ct[b] * pltpu.roll(y, total - b, 1)[:, 0:length]
-        here = pl.ds(pl.multiple_of(r * rows, rows), rows)
-        diff[0, here, :] = before[0, here, :] - z
+        mid[pl.ds(pl.multiple_of(r * rows, rows), rows), :] = y
         return carry
 
     lax.fori_loop(0, height // rows, step, 0)
+    shape = (4 * LANES, 2 * LANES)
+    tap = lax.broadcasted_iota(jnp.int32, shape, 0) - lax.broadcasted_iota(jnp.int32, shape, 1) - turn
+    taps = jnp.zeros(shape, F32)
+    for b in range(4):
+        taps = jnp.where(tap == b, ct[b], taps)
+    t_high, t_low = split2(taps)
+    high, low = split2(mid[...])
+    both = jnp.concatenate([high, low], axis=0)
+    for begin in range(0, length, 2 * LANES):
+        window = slice(begin, begin + 4 * LANES)
+        two = jnp.dot(both[:, window], t_high, preferred_element_type=F32)
+        z = two[:height] + two[height:] + jnp.dot(
+            high[:, window], t_low, preferred_element_type=F32
+        )
+        here = slice(begin, begin + 2 * LANES)
+        diff[0, :, here] = before[0, :, here] - z
     high, low = split2(diff[0])
     rr = r_tab[0]
     pr = rr.shape[0] // 2
@@ -536,16 +598,19 @@
     ).transpose(0, 2, 1)
     struct = jax.ShapeDtypeStruct
     dma = pltpu.SemaphoreType.DMA
-    ends, flanks, slots = pl.pallas_call(
+    ends, flanks, slots, _ = pl.pallas_call(
         functools.partial(halo_kernel, n_row, n_col),
         out_shape=(
             struct((2, scans, HALO, width), F32),
             struct((2, scans, height, LANES), F32),
             struct((6, scans, 8, height), F32),
+            struct((scans - scans // 2, HALO, length), F32),
         ),
         in_specs=[ANY, ANY],
-        out_specs=(ANY, ANY, ANY),
-        scratch_shapes=[dma((8, scans)), dma((8, scans)), dma((6,)), dma((6,))],
+        out_specs=(ANY, ANY, ANY, ANY),
+        scratch_shapes=[
+            dma((8, scans)), dma((8, scans)), dma((6,)), dma((6,)), dma((scans,)), dma((scans,))
+        ],
         compiler_params=pltpu.CompilerParams(
             collective_id=0, has_side_effects=True, vmem_limit_bytes=VMEM_LIMIT
         ),
@@ -557,7 +622,7 @@
     row_part = lambda s, p, *_: (p[0], 0, 0)
     col_part = lambda s, p, *_: (p[1], 0, 0)
     diff, partial, edges = pl.pallas_call(
-        shift_kernel,
+        functools.partial(shift_kernel, n_col),
         out_shape=(
             struct((scans, height, length), F32),
             struct((n_col, scans, pr, LANES), F32),
@@ -581,11 +646,14 @@
                 pl.BlockSpec((n_col, 1, pr, LANES), all_scan),
                 pl.BlockSpec((1, 2 * EDGE, height), by_scan),
             ),
-            scratch_shapes=[pltpu.VMEM((height + 2 * HALO, width + LANES), F32)],
+            scratch_shapes=[
+                pltpu.VMEM((height + 2 * HALO, width + 2 * LANES), F32),
+                pltpu.VMEM((height, width), F32),
+            ],
         ),
         compiler_params=pltpu.CompilerParams(vmem_limit_bytes=VMEM_LIMIT),
         name="shift",
-    )(place, offsets[:, :, 0, 0], fractions[:, :, 0, 0], after, ends, flanks, before, slots, r_tab, c_tab, hc)
+    )(place, offsets, fractions, after, ends, flanks, before, slots, r_tab, c_tab, hc)
 
     rows_out, corners, sides, spread = pl.pallas_call(
         functools.partial(gather_kernel, n_row, n_col),

time: 140 us -> 127 us (0.907)
  Pallas kernels: 134 us -> 118 us
  local copies, waits for them, and re-layouts: 3.98 us -> 6.68 us
    pallas_call x1, Pallas kernels: 51.5 us -> 24.8 us  [body(): pl.pallas_call(functools.partial(gather_kernel, n_row, n_col), out_shape=...]
    pallas_call x1, Pallas kernels: 25.4 us -> 39.1 us  [body(): pl.pallas_call(functools.partial(halo_kernel, n_row, n_col), out_shape=(s...]
    pallas_call x1, Pallas kernels: 21.6 us -> 18 us  [body(): pl.pallas_call(functools.partial(shift_kernel, n_col), out_shape=(struct(...]
    unnamed x3 -> x5, local copies, waits for them, and re-layouts: 1.57 us -> 4.27 us
where the time goes in v3:
time: 127 us
  Pallas kernels  118 us (93%)
  local copies, waits for them, and re-layouts  6.68 us (5%)
  other arithmetic  1.29 us (1%)
    pallas_call x1, Pallas kernels, body(): pl.pallas_call(functools.partial(halo_kernel, n_row, n_col), out_shape=(s...  39.1 us
    pallas_call x1, Pallas kernels, body(): pl.pallas_call(functools.partial(band_kernel, n_row, n_col), out_shape=(s...  25.2 us
    pallas_call x1, Pallas kernels, body(): pl.pallas_call(functools.partial(gather_kernel, n_row, n_col), out_shape=...  24.8 us
    pallas_call x1, Pallas kernels, body(): pl.pallas_call(functools.partial(shift_kernel, n_col), out_shape=(struct(...  18 us
    pallas_call x1, Pallas kernels, body(): pl.pallas_call(functools.partial(total_kernel, n_row, n_col, float(n_row...  11.1 us
    unnamed x5, local copies, waits for them, and re-layouts  4.27 us

profile of v3, /device:TPU:0, one launch (start us, length us, event | category | flops | bytes accessed | tf_op | source)
XLA Modules:
  0.0 126.8 jit_solution(13162956250463482340)
XLA Ops:
  0.6 0.6 pad_add_fusion.place
  1.2 0.1 pad.1.clone
  1.3 1.3 %copy.17.offsets = s32[2,4,1,1]{3,2,1,0:T(1,128)} copy(s32[2,4,1,1]{1,3,2,0:T(1,128)} %param.14) | data formatting | bytes 64 | tf_op args[2]
  2.6 1.4 %copy.18.fractions = s32[2,4,1,1]{3,2,1,0:T(1,128)} copy(s32[2,4,1,1]{1,3,2,0:T(1,128)} %param.15) | data formatting | bytes 64 | tf_op args[3]
  4.0 1.1 slice.6
  5.1 0.2 copy.19
  5.3 1.3 slice.7
  6.5 0.2 copy.20
  6.7 0.7 maximum_bitcast_fusion.extra
  7.4 39.1 %halo.1 = (f32[2,4,136,1280]{3,2,1,0:T(8,128)}, f32[2,4,256,128]{3,2,1,0:T(8,128)}, f32[6,4,8,256]{3,2,1,0:T(8,128)}, f32[2,136,1024]{2,1,0:T(8,128)}) custom-call(f32[4,256,1024]{2,1,0:T(8,128)} %after.3, f32[4,8,256]{2,1,0:T(8,128)} %maximum_bitcast_fusion.extra), custom_call_target="tpu_custom_call" | custom-call | tf_op jit(solution)/shard_map/halo/pallas_call | solution.py:601
  46.5 18.0 %shift.1 = (f32[4,256,1024]{2,1,0:T(8,128)}, f32[4,4,24,128]{3,2,1,0:T(8,128)}, f32[4,16,256]{2,1,0:T(8,128)}) custom-call(s32[2]{0:T(128)} %pad_add_fusion.place, s32[2,4,1,1]{3,2,1,0:T(1,128)} %copy.17.offsets, s32[2,4,1,1]{3,2,1,0:T(1,128)} %copy.18.fractions, f32[4,256,1024]{2,1,0:T(8,128)} %after.3, f32[2,4,136,1280]{3,2,1,0:T(8,128)} %get-tuple-element.16.ends, ...), custom_call_target="tpu_custom_call" | custom-call | tf_op jit(solution)/shard_map/shift/pallas_call | solution.py:624
  64.5 24.8 %gather.1 = (f32[2,4,8,1024]{3,2,1,0:T(8,128)}, f32[4,4,8,128]{3,2,1,0:T(8,128)}, f32[2,4,8,256]{3,2,1,0:T(8,128)}, f32[8,4,24,128]{3,2,1,0:T(8,128)}) custom-call(f32[4,256,1024]{2,1,0:T(8,128)} %get-tuple-element.19.diff, f32[4,4,24,128]{3,2,1,0:T(8,128)} %get-tuple-element.20.partial, f32[4,16,256]{2,1,0:T(8,128)} %get-tuple-element.21.edges), custom_call_target="tpu_custom_call" | custom-call | tf_op jit(solution)/shard_map/gather/pallas_call | solution.py:658
  89.3 25.2 %band.1 = (f32[4,256,1024]{2,1,0:T(8,128)}, f32[4,256,1024]{2,1,0:T(8,128)}, f32[4,2,8,128]{3,2,1,0:T(8,128)}) custom-call(s32[2]{0:T(128)} %pad_add_fusion.place, f32[4,256,1024]{2,1,0:T(8,128)} %get-tuple-element.19.diff, f32[2,4,8,1024]{3,2,1,0:T(8,128)} %get-tuple-element.22.rows_in, f32[4,4,8,128]{3,2,1,0:T(8,128)} %get-tuple-element.23.corners, ...), custom_call_target="tpu_custom_call" | custom-call | tf_op jit(solution)/shard_map/band/pallas_call | solution.py:679
  114.5 11.1 %total.1 = f32[2,4]{1,0:T(2,128)} custom-call(f32[4,2,8,128]{3,2,1,0:T(8,128)} %get-tuple-element.28.sums), custom_call_target="tpu_custom_call" | custom-call | tf_op jit(solution)/shard_map/total/pallas_call | solution.py:711
  125.6 1.2 copy.22
  (1 shorter events, 0.0 us)

commit v4 on v3

--- a/solution.py
+++ b/solution.py
@@ -179,10 +179,21 @@
     return found
 
 
-def halo_kernel(n_row, n_col, after, extra, ends, flanks, slots, via, send, recv, slot_send, slot_recv,
-                via_send, via_recv):
+def shift_kernel(n_row, n_col, drift, after, before_in, extra, r_in, c_in, h_in, diff, partial, edges,
+                 ends, flanks, slots, via, own, before, r_tab, c_tab, h_tab, wide, mid,
+                 send, recv, slot_send, slot_recv, via_send, via_recv, load):
     scans, height, length = after.shape
     near = neighbours(n_row, n_col)
+    here = (lax.axis_index("row"), lax.axis_index("col"))
+    loads = [
+        pltpu.make_async_copy(src, dst, load.at[k])
+        for k, (src, dst) in enumerate((
+            (after, own), (before_in, before), (r_in.at[here[0]], r_tab),
+            (c_in.at[here[1]], c_tab), (h_in.at[here[1]], h_tab),
+        ))
+    ]
+    for copy in loads:
+        copy.start()
     barrier = pltpu.get_barrier_semaphore()
     count = jnp.int32(0)
     for exists, device in near.values():
@@ -248,6 +259,9 @@
     def when(pred, action):
         pl.when(pred)(action)
 
+    for dc in (1, -1):
+        for dr in (-1, 0, 1):
+            when(near[dr, dc][0], slot_copy(dr, dc).start)
     for s in relayed:
         for dr in (1, -1):
             when(row == routes[dr][0], first_leg(s, dr).start)
@@ -260,19 +274,39 @@
     for s in range(scans):
         for dc in (1, -1):
             when(near[0, dc][0], col_copy(s, dc, 0).start)
-    for dc in (1, -1):
-        for dr in (-1, 0, 1):
-            when(near[dr, dc][0], slot_copy(dr, dc).start)
     for s in relayed:
         for dr in (1, -1):
             when(row == routes[dr][1], first_leg(s, dr).wait_recv)
             when(row == routes[dr][1], second_leg(s, dr).start)
-    for s in range(scans):
-        for dr in (1, -1):
-            source = near[-dr, 0][0]
-            when(source, row_copy(s, dr).wait_recv)
+    for copy in loads:
+        copy.wait()
+    for dc in (1, -1):
+        for dr in (-1, 0, 1):
+            when(near[-dr, -dc][0], slot_copy(dr, dc).wait_recv)
+
+    def step(t, carry):
+        @pl.when(t < scans)
+        def _():
+            for dr in (1, -1):
+                source = near[-dr, 0][0]
+                when(source, row_copy(t, dr).wait_recv)
+                for dc in (1, -1):
+                    when(source & near[0, dc][0], col_copy(t, dc, -dr).start)
+
+        @pl.when(t > 0)
+        def _():
             for dc in (1, -1):
-                when(source & near[0, dc][0], col_copy(s, dc, -dr).start)
+                for band in (-1, 0, 1):
+                    ok = jnp.bool_(True) if band == 0 else near[band, 0][0]
+                    when(ok & near[0, -dc][0], col_copy(t - 1, dc, band).wait_recv)
+            shift_scan(
+                n_row, n_col, t - 1, drift, own, ends, flanks, before, slots, r_tab, c_tab, h_tab,
+                diff, partial, edges, wide, mid,
+            )
+
+        return carry
+
+    lax.fori_loop(0, scans + 1, step, 0)
     for s in range(scans):
         for dr in (1, -1):
             when(near[dr, 0][0], row_copy(s, dr).wait_send)
@@ -280,14 +314,12 @@
             for band in (-1, 0, 1):
                 ok = jnp.bool_(True) if band == 0 else near[band, 0][0]
                 when(ok & near[0, dc][0], col_copy(s, dc, band).wait_send)
-                when(ok & near[0, -dc][0], col_copy(s, dc, band).wait_recv)
     for s in relayed:
         for dr in (1, -1):
             when(row == routes[dr][1], second_leg(s, dr).wait_send)
     for dc in (1, -1):
         for dr in (-1, 0, 1):
             when(near[dr, dc][0], slot_copy(dr, dc).wait_send)
-            when(near[-dr, -dc][0], slot_copy(dr, dc).wait_recv)
 
 
 def split2(value):
@@ -314,16 +346,18 @@
     )
 
 
-def shift_kernel(n_col, place, offsets, fractions, after, ends, flanks, before, slots, r_tab, c_tab,
-                 h_tab, diff, partial, edges, wide, mid):
-    s = pl.program_id(0)
-    height, length = before.shape[1], before.shape[2]
+def shift_scan(n_row, n_col, s, drift, after, ends, flanks, before, slots, r_tab, c_tab, h_tab,
+               diff, partial, edges, wide, mid):
+    scans, height, length = before.shape
     width = length + 2 * LANES
-    dr, dc = offsets[0, s, 0, 0], offsets[1, s, 0, 0]
-    rt = cubic(fractions[0, s, 0, 0].astype(F32) / 256.0)
-    ct = cubic(fractions[1, s, 0, 0].astype(F32) / 256.0)
+    dr, dc = drift[s], drift[scans + s]
+    rt = cubic(drift[2 * scans + s].astype(F32) / 256.0)
+    ct = cubic(drift[3 * scans + s].astype(F32) / 256.0)
+    col = lax.axis_index("col")
     zero = jnp.float32(0.0)
-    has_left, has_right = place[1] > 0, place[1] < n_col - 1
+    row = lax.axis_index("row")
+    has_left, has_right = col > 0, col < n_col - 1
+    has_rows = (row > 0, jnp.bool_(True), row < n_row - 1)
     first, last = slice(0, LANES), slice(length + 3 * LANES, length + 4 * LANES)
     left, inner = slice(LANES, 2 * LANES), slice(2 * LANES, 2 * LANES + length)
     right = slice(2 * LANES + length, 3 * LANES + length)
@@ -334,62 +368,53 @@
         (slice(HALO + height, height + 2 * HALO), slice(0, HALO)),
     )
     for j, (here, part) in enumerate(spans):
-        low = jnp.transpose(jnp.concatenate([blank, slots[j, 0]], axis=0))
-        high = jnp.transpose(jnp.concatenate([slots[3 + j, 0], blank], axis=0))
-        wide[here, first] = jnp.where(has_left, low[part], zero)
-        wide[here, last] = jnp.where(has_right, high[part], zero)
+        low = jnp.transpose(jnp.concatenate([blank, slots[j, s]], axis=0))
+        high = jnp.transpose(jnp.concatenate([slots[3 + j, s], blank], axis=0))
+        wide[here, first] = jnp.where(has_left & has_rows[j], low[part], zero)
+        wide[here, last] = jnp.where(has_right & has_rows[j], high[part], zero)
     for v in range(2):
         here = spans[2 * v][0]
-        wide[here, left] = jnp.where(has_left, ends[v, 0, :, 0:LANES], zero)
-        wide[here, inner] = ends[v, 0, :, LANES : LANES + length]
-        wide[here, right] = jnp.where(has_right, ends[v, 0, :, LANES + length :], zero)
+        found = has_rows[2 * v]
+        wide[here, left] = jnp.where(has_left & found, ends[v, s, :, 0:LANES], zero)
+        wide[here, inner] = jnp.where(found, ends[v, s, :, LANES : LANES + length], zero)
+        wide[here, right] = jnp.where(has_right & found, ends[v, s, :, LANES + length :], zero)
     here = spans[1][0]
-    wide[here, left] = jnp.where(has_left, flanks[0, 0], zero)
-    wide[here, inner] = after[0]
-    wide[here, right] = jnp.where(has_right, flanks[1, 0], zero)
-    start = HALO - 1 + dr
-    lane = 2 * LANES - 1 + dc
-    lane_base = pl.multiple_of((lane // LANES) * LANES, LANES)
-    turn = lane - lane_base
-    rows = 32
-
-    def step(r, carry):
-        top = start + r * rows
-        base = pl.multiple_of((top // 8) * 8, 8)
-        off = top - base
-        x = wide[pl.ds(base, rows + 16), pl.ds(lane_base, width)]
-        x = pltpu.roll(x, lax.rem(rows + 16 - off, rows + 16), 0)
-        y = rt[0] * x[0:rows] + rt[1] * x[1 : rows + 1] + rt[2] * x[2 : rows + 2] + rt[3] * x[3 : rows + 3]
-        mid[pl.ds(pl.multiple_of(r * rows, rows), rows), :] = y
-        return carry
-
-    lax.fori_loop(0, height // rows, step, 0)
-    shape = (4 * LANES, 2 * LANES)
-    tap = lax.broadcasted_iota(jnp.int32, shape, 0) - lax.broadcasted_iota(jnp.int32, shape, 1) - turn
-    taps = jnp.zeros(shape, F32)
-    for b in range(4):
-        taps = jnp.where(tap == b, ct[b], taps)
-    t_high, t_low = split2(taps)
+    wide[here, left] = jnp.where(has_left, flanks[0, s], zero)
+    wide[here, inner] = after[s]
+    wide[here, right] = jnp.where(has_right, flanks[1, s], zero)
+    def taps_at(shape, axis, offset, weights):
+        tap = lax.broadcasted_iota(jnp.int32, shape, axis)
+        tap = tap - lax.broadcasted_iota(jnp.int32, shape, 1 - axis) - offset
+        taps = jnp.zeros(shape, F32)
+        for b in range(4):
+            taps = jnp.where(tap == b, weights[b], taps)
+        return split2(taps)
+
+    t_high, t_low = taps_at((height, height + 2 * HALO), 1, HALO - 1 + dr, rt)
+    high, low = split2(wide[...])
+    two = jnp.dot(jnp.concatenate([t_high, t_low], axis=0), high, preferred_element_type=F32)
+    mid[...] = two[:height] + two[height:] + jnp.dot(t_high, low, preferred_element_type=F32)
+    t_high, t_low = taps_at((6 * LANES, 2 * LANES), 0, 2 * LANES - 1 + dc, ct)
     high, low = split2(mid[...])
     both = jnp.concatenate([high, low], axis=0)
     for begin in range(0, length, 2 * LANES):
-        window = slice(begin, begin + 4 * LANES)
+        window = slice(begin, begin + 6 * LANES)
         two = jnp.dot(both[:, window], t_high, preferred_element_type=F32)
         z = two[:height] + two[height:] + jnp.dot(
             high[:, window], t_low, preferred_element_type=F32
         )
         here = slice(begin, begin + 2 * LANES)
-        diff[0, :, here] = before[0, :, here] - z
-    high, low = split2(diff[0])
-    rr = r_tab[0]
+        diff[s, :, here] = before[s, :, here] - z
+    high, low = split2(diff[s])
+    rr = r_tab[...]
     pr = rr.shape[0] // 2
     both = jnp.dot(rr, high, preferred_element_type=F32)
     mixed = both[:pr] + both[pr:] + jnp.dot(rr[:pr], low, preferred_element_type=F32)
-    here = jnp.dot(mixed, c_tab[0], precision=HIGHEST, preferred_element_type=F32)
+    here = jnp.dot(mixed, c_tab[...], precision=HIGHEST, preferred_element_type=F32)
     for t in range(partial.shape[0]):
-        partial[t, 0] = jnp.dot(here, h_tab[0, t], precision=HIGHEST, preferred_element_type=F32)
-    edges[0, 0:EDGE] = jnp.transpose(diff[0, :, 0:LANES])[0:EDGE]
-    edges[0, EDGE:] = jnp.transpose(diff[0, :, length - LANES :])[LANES - EDGE :]
+        partial[t, s] = jnp.dot(here, h_tab[t], precision=HIGHEST, preferred_element_type=F32)
+    edges[s, 0:EDGE] = jnp.transpose(diff[s, :, 0:LANES])[0:EDGE]
+    edges[s, EDGE:] = jnp.transpose(diff[s, :, length - LANES :])[LANES - EDGE :]
 
 
 def gather_kernel(n_row, n_col, diff, partial, edges, rows_out, corners, sides, spread, parts,
@@ -470,7 +495,9 @@
     tall = height + 2 * EDGE
     zero = jnp.float32(0.0)
     has_top, has_bottom = row > 0, row < n_row - 1
+    row = lax.axis_index("row")
     has_left, has_right = col > 0, col < n_col - 1
+    has_rows = (row > 0, jnp.bool_(True), row < n_row - 1)
     mid = slice(LANES, LANES + length)
     x[EDGE : EDGE + height, mid] = diff[0]
     x[0:EDGE, mid] = jnp.where(has_top, rows_in[0, 0], zero)
@@ -598,63 +625,42 @@
     ).transpose(0, 2, 1)
     struct = jax.ShapeDtypeStruct
     dma = pltpu.SemaphoreType.DMA
-    ends, flanks, slots, _ = pl.pallas_call(
-        functools.partial(halo_kernel, n_row, n_col),
-        out_shape=(
-            struct((2, scans, HALO, width), F32),
-            struct((2, scans, height, LANES), F32),
-            struct((6, scans, 8, height), F32),
-            struct((scans - scans // 2, HALO, length), F32),
-        ),
-        in_specs=[ANY, ANY],
-        out_specs=(ANY, ANY, ANY, ANY),
-        scratch_shapes=[
-            dma((8, scans)), dma((8, scans)), dma((6,)), dma((6,)), dma((scans,)), dma((scans,))
-        ],
-        compiler_params=pltpu.CompilerParams(
-            collective_id=0, has_side_effects=True, vmem_limit_bytes=VMEM_LIMIT
-        ),
-        name="halo",
-    )(after, extra)
-
-    all_scan = lambda s, *_: (0, s, 0, 0)
-    by_scan = lambda s, *_: (s, 0, 0)
-    row_part = lambda s, p, *_: (p[0], 0, 0)
-    col_part = lambda s, p, *_: (p[1], 0, 0)
+    smem = pl.BlockSpec(memory_space=pltpu.SMEM)
+    drift = jnp.concatenate([offsets.reshape(2 * scans), fractions.reshape(2 * scans)])
     diff, partial, edges = pl.pallas_call(
-        functools.partial(shift_kernel, n_col),
+        functools.partial(shift_kernel, n_row, n_col),
         out_shape=(
             struct((scans, height, length), F32),
             struct((n_col, scans, pr, LANES), F32),
             struct((scans, 2 * EDGE, height), F32),
         ),
-        grid_spec=pltpu.PrefetchScalarGridSpec(
-            num_scalar_prefetch=3,
-            grid=(scans,),
-            in_specs=[
-                pl.BlockSpec((1, height, length), by_scan),
-                pl.BlockSpec((2, 1, HALO, width), all_scan),
-                pl.BlockSpec((2, 1, height, LANES), all_scan),
-                pl.BlockSpec((1, height, length), by_scan),
-                pl.BlockSpec((6, 1, 8, height), lambda s, *_: (0, s, 0, 0)),
-                pl.BlockSpec((1, 2 * pr, height), row_part),
-                pl.BlockSpec((1, length, LANES), col_part),
-                pl.BlockSpec((1, n_col, LANES, LANES), lambda s, p, *_: (p[1], 0, 0, 0)),
-            ],
-            out_specs=(
-                pl.BlockSpec((1, height, length), by_scan),
-                pl.BlockSpec((n_col, 1, pr, LANES), all_scan),
-                pl.BlockSpec((1, 2 * EDGE, height), by_scan),
-            ),
-            scratch_shapes=[
-                pltpu.VMEM((height + 2 * HALO, width + 2 * LANES), F32),
-                pltpu.VMEM((height, width), F32),
-            ],
+        in_specs=[smem, ANY, ANY, VM, ANY, ANY, ANY],
+        out_specs=(VM, VM, VM),
+        scratch_shapes=[
+            pltpu.VMEM((2, scans, HALO, width), F32),
+            pltpu.VMEM((2, scans, height, LANES), F32),
+            pltpu.VMEM((6, scans, 8, height), F32),
+            pltpu.VMEM((scans - scans // 2, HALO, length), F32),
+            pltpu.VMEM((scans, height, length), F32),
+            pltpu.VMEM((scans, height, length), F32),
+            pltpu.VMEM(r_tab.shape[1:], BF16),
+            pltpu.VMEM(c_tab.shape[1:], F32),
+            pltpu.VMEM(hc.shape[1:], F32),
+            pltpu.VMEM((height + 2 * HALO, width + 2 * LANES), F32),
+            pltpu.VMEM((height, width + 2 * LANES), F32),
+            dma((8, scans)), dma((8, scans)), dma((6,)), dma((6,)), dma((scans,)), dma((scans,)),
+            dma((5,)),
+        ],
+        compiler_params=pltpu.CompilerParams(
+            collective_id=0, has_side_effects=True, vmem_limit_bytes=VMEM_LIMIT
         ),
-        compiler_params=pltpu.CompilerParams(vmem_limit_bytes=VMEM_LIMIT),
         name="shift",
-    )(place, offsets, fractions, after, ends, flanks, before, slots, r_tab, c_tab, hc)
-
+    )(drift, after, before, extra, r_tab, c_tab, hc)
+
+    all_scan = lambda s, *_: (0, s, 0, 0)
+    by_scan = lambda s, *_: (s, 0, 0)
+    row_part = lambda s, p, *_: (p[0], 0, 0)
+    col_part = lambda s, p, *_: (p[1], 0, 0)
     rows_out, corners, sides, spread = pl.pallas_call(
         functools.partial(gather_kernel, n_row, n_col),
         out_shape=(

time: 127 us -> 118 us (0.929)
  Pallas kernels: 118 us -> 108 us
  other arithmetic: 1.29 us -> 4.58 us
  local copies, waits for them, and re-layouts: 6.68 us -> 4.7 us
    pallas_call x2 -> x1, Pallas kernels: 57.1 us -> 43.6 us  [body(): pl.pallas_call(functools.partial(shift_kernel, n_row, n_col), out_shape=(...]
    unnamed x0 -> x2, other arithmetic: none -> 2.68 us
    pallas_call x1, Pallas kernels: 24.8 us -> 27.4 us  [body(): pl.pallas_call(functools.partial(gather_kernel, n_row, n_col), out_shape=...]
    unnamed x5 -> x4, local copies, waits for them, and re-layouts: 4.27 us -> 2.13 us
where the time goes in v4:
time: 118 us
  Pallas kernels  108 us (92%)
  local copies, waits for them, and re-layouts  4.7 us (4%)
  other arithmetic  4.58 us (4%)
    pallas_call x1, Pallas kernels, body(): pl.pallas_call(functools.partial(shift_kernel, n_row, n_col), out_shape=(...  43.6 us
    pallas_call x1, Pallas kernels, body(): pl.pallas_call(functools.partial(gather_kernel, n_row, n_col), out_shape=...  27.4 us
    pallas_call x1, Pallas kernels, body(): pl.pallas_call(functools.partial(band_kernel, n_row, n_col), out_shape=(s...  25.2 us
    pallas_call x1, Pallas kernels, body(): pl.pallas_call(functools.partial(total_kernel, n_row, n_col, float(n_row...  11.5 us
    unnamed x2, other arithmetic  2.68 us

profile of v4, /device:TPU:0, one launch (start us, length us, event | category | flops | bytes accessed | tf_op | source)
XLA Modules:
  0.0 117.6 jit_solution(12070200487176127959)
XLA Ops:
  0.6 0.6 pad_add_fusion.place
  1.2 0.1 pad.1.clone
  1.3 0.5 broadcast.8
  1.8 1.3 %reduce.7 = s32[2,4]{1,0:T(2,128)S(1)} reduce(s32[2,4,1,1]{1,3,2,0:T(1,128)} %param.14, s32[]{:T(128)} %broadcast.8), dimensions={2,3}, to_apply=%param.14.reduce_sub_computation.3 | reduce | bytes 68 | tf_op args[2]
  3.2 0.1 reshape.12
  3.3 1.3 %reduce.6 = s32[2,4]{1,0:T(2,128)S(1)} reduce(s32[2,4,1,1]{1,3,2,0:T(1,128)} %param.15, s32[]{:T(128)} %broadcast.8), dimensions={2,3}, to_apply=%param.15.reduce_sub_computation.3 | reduce | bytes 68 | tf_op args[3]
  4.6 0.1 reshape.13
  4.7 0.6 pad_add_fusion.1.drift
  5.3 1.1 slice.6
  6.4 0.2 copy.17
  6.5 1.3 %slice.7 = f32[4,256,1]{2,1,0:T(8,128)S(1)} slice(f32[4,256,1024]{2,1,0:T(8,128)} %after.1), slice={[0:4], [0:256], [895:896]} | slice | bytes 8192 | tf_op jit(solution)/shard_map/slice | solution.py:624
  7.8 0.2 copy.18
  8.0 0.7 maximum_bitcast_fusion.extra
  8.7 43.6 %shift.1 = (f32[4,256,1024]{2,1,0:T(8,128)}, f32[4,4,24,128]{3,2,1,0:T(8,128)}, f32[4,16,256]{2,1,0:T(8,128)}) custom-call(s32[16]{0:T(128)} %pad_add_fusion.1.drift, f32[4,256,1024]{2,1,0:T(8,128)} %after.1, f32[4,256,1024]{2,1,0:T(8,128)} %before_in.1, f32[4,8,256]{2,1,0:T(8,128)} %maximum_bitcast_fusion.extra, bf16[8,48,256]{2,1,0:T(8,128)(2,1)} %constant.27.clone.r_in, ...), custom_call_target="tpu_custom_call" | custom-call | tf_op jit(solution)/shard_map/shift/pallas_call | solution.py:630
  52.3 27.4 %gather.1 = (f32[2,4,8,1024]{3,2,1,0:T(8,128)}, f32[4,4,8,128]{3,2,1,0:T(8,128)}, f32[2,4,8,256]{3,2,1,0:T(8,128)}, f32[8,4,24,128]{3,2,1,0:T(8,128)}) custom-call(f32[4,256,1024]{2,1,0:T(8,128)} %get-tuple-element.13.diff, f32[4,4,24,128]{3,2,1,0:T(8,128)} %get-tuple-element.14.partial, f32[4,16,256]{2,1,0:T(8,128)} %get-tuple-element.15.edges), custom_call_target="tpu_custom_call" | custom-call | tf_op jit(solution)/shard_map/gather/pallas_call | solution.py:664
  79.6 25.2 %band.1 = (f32[4,256,1024]{2,1,0:T(8,128)}, f32[4,256,1024]{2,1,0:T(8,128)}, f32[4,2,8,128]{3,2,1,0:T(8,128)}) custom-call(s32[2]{0:T(128)} %pad_add_fusion.place, f32[4,256,1024]{2,1,0:T(8,128)} %get-tuple-element.13.diff, f32[2,4,8,1024]{3,2,1,0:T(8,128)} %get-tuple-element.16.rows_in, f32[4,4,8,128]{3,2,1,0:T(8,128)} %get-tuple-element.17.corners, ...), custom_call_target="tpu_custom_call" | custom-call | tf_op jit(solution)/shard_map/band/pallas_call | solution.py:685
  104.8 11.5 %total.1 = f32[2,4]{1,0:T(2,128)} custom-call(f32[4,2,8,128]{3,2,1,0:T(8,128)} %get-tuple-element.22.sums), custom_call_target="tpu_custom_call" | custom-call | tf_op jit(solution)/shard_map/total/pallas_call | solution.py:717
  116.4 1.2 %copy.20 = f32[2,4]{1,0:T(2,128)} copy(f32[2,4]{1,0:T(2,128)} %total.1) | data formatting | bytes 64
  (1 shorter events, 0.0 us)

commit v5 on v4

--- a/solution.py
+++ b/solution.py
@@ -179,8 +179,8 @@
     return found
 
 
-def shift_kernel(n_row, n_col, drift, after, before_in, extra, r_in, c_in, h_in, diff, partial, edges,
-                 ends, flanks, slots, via, own, before, r_tab, c_tab, h_tab, wide, mid,
+def shift_kernel(n_row, n_col, offsets, fractions, after, before_in, r_in, c_in, h_in, diff, partial, edges,
+                 ends, flanks, slots, via, extra, own, before, r_tab, c_tab, h_tab, wide, mid,
                  send, recv, slot_send, slot_recv, via_send, via_recv, load):
     scans, height, length = after.shape
     near = neighbours(n_row, n_col)
@@ -215,6 +215,10 @@
                 for other in others:
                     signal(barrier, (other, col))
 
+    loads[0].wait()
+    for s in range(scans):
+        extra[s] = jnp.transpose(own[s, :, LANES : 2 * LANES])[0:8]
+        extra[s, 7:8] = jnp.transpose(own[s, :, length - 2 * LANES : length - LANES])[LANES - 1 :]
     pl.semaphore_wait(barrier, count)
 
     def row_copy(s, dr):
@@ -278,7 +282,7 @@
         for dr in (1, -1):
             when(row == routes[dr][1], first_leg(s, dr).wait_recv)
             when(row == routes[dr][1], second_leg(s, dr).start)
-    for copy in loads:
+    for copy in loads[1:]:
         copy.wait()
     for dc in (1, -1):
         for dr in (-1, 0, 1):
@@ -300,7 +304,7 @@
                     ok = jnp.bool_(True) if band == 0 else near[band, 0][0]
                     when(ok & near[0, -dc][0], col_copy(t - 1, dc, band).wait_recv)
             shift_scan(
-                n_row, n_col, t - 1, drift, own, ends, flanks, before, slots, r_tab, c_tab, h_tab,
+                n_row, n_col, t - 1, offsets, fractions, own, ends, flanks, before, slots, r_tab, c_tab, h_tab,
                 diff, partial, edges, wide, mid,
             )
 
@@ -327,14 +331,6 @@
     return high, (value - high.astype(F32)).astype(BF16)
 
 
-def split3(value):
-    a = value.astype(BF16)
-    rest = value - a.astype(F32)
-    b = rest.astype(BF16)
-    c = (rest - b.astype(F32)).astype(BF16)
-    return a, b, c
-
-
 def cubic(t):
     t2 = t * t
     t3 = t2 * t
@@ -346,13 +342,13 @@
     )
 
 
-def shift_scan(n_row, n_col, s, drift, after, ends, flanks, before, slots, r_tab, c_tab, h_tab,
+def shift_scan(n_row, n_col, s, offsets, fractions, after, ends, flanks, before, slots, r_tab, c_tab, h_tab,
                diff, partial, edges, wide, mid):
     scans, height, length = before.shape
     width = length + 2 * LANES
-    dr, dc = drift[s], drift[scans + s]
-    rt = cubic(drift[2 * scans + s].astype(F32) / 256.0)
-    ct = cubic(drift[3 * scans + s].astype(F32) / 256.0)
+    dr, dc = offsets[0, 0, 0, s], offsets[1, 0, 0, s]
+    rt = cubic(fractions[0, 0, 0, s].astype(F32) / 256.0)
+    ct = cubic(fractions[1, 0, 0, s].astype(F32) / 256.0)
     col = lax.axis_index("col")
     zero = jnp.float32(0.0)
     row = lax.axis_index("row")
@@ -532,9 +528,9 @@
     smooth = two[:tall] + two[tall:] + jnp.dot(gr[0, :tall], low, preferred_element_type=F32)
     q = jnp.concatenate([spread[i, 0] for i in range(n_row)], axis=0)
     mixed = jnp.dot(ru[0], q, precision=HIGHEST, preferred_element_type=F32)
-    pieces = jnp.concatenate(split3(mixed), axis=1)
+    pieces = jnp.concatenate(split2(mixed), axis=1)
     cub = cu[0].astype(BF16)
-    wavy = jnp.dot(pieces, jnp.concatenate([cub, cub, cub], axis=0), preferred_element_type=F32)
+    wavy = jnp.dot(pieces, jnp.concatenate([cub, cub], axis=0), preferred_element_type=F32)
     b[...] = smooth - wavy
 
     lane = lax.broadcasted_iota(jnp.int32, (1, length), 1) + col * length
@@ -619,14 +615,10 @@
     c_tab, hc, cu, ru, cw, r_tab, gc, gr = tables(n_row * height, n_col * length, height, length)
     pr = r_tab.shape[1] // 2
     place = jnp.stack([lax.axis_index("row"), lax.axis_index("col")]).astype(jnp.int32)
-    filler = jnp.zeros((scans, height, 5), F32)
-    extra = jnp.concatenate(
-        [after[:, :, LANES : LANES + 2], filler, after[:, :, length - LANES - 1 : length - LANES]], axis=2
-    ).transpose(0, 2, 1)
     struct = jax.ShapeDtypeStruct
     dma = pltpu.SemaphoreType.DMA
     smem = pl.BlockSpec(memory_space=pltpu.SMEM)
-    drift = jnp.concatenate([offsets.reshape(2 * scans), fractions.reshape(2 * scans)])
+    scan_last = (0, 2, 3, 1)
     diff, partial, edges = pl.pallas_call(
         functools.partial(shift_kernel, n_row, n_col),
         out_shape=(
@@ -634,13 +626,14 @@
             struct((n_col, scans, pr, LANES), F32),
             struct((scans, 2 * EDGE, height), F32),
         ),
-        in_specs=[smem, ANY, ANY, VM, ANY, ANY, ANY],
+        in_specs=[smem, smem, ANY, ANY, ANY, ANY, ANY],
         out_specs=(VM, VM, VM),
         scratch_shapes=[
             pltpu.VMEM((2, scans, HALO, width), F32),
             pltpu.VMEM((2, scans, height, LANES), F32),
             pltpu.VMEM((6, scans, 8, height), F32),
             pltpu.VMEM((scans - scans // 2, HALO, length), F32),
+            pltpu.VMEM((scans, 8, height), F32),
             pltpu.VMEM((scans, height, length), F32),
             pltpu.VMEM((scans, height, length), F32),
             pltpu.VMEM(r_tab.shape[1:], BF16),
@@ -655,7 +648,7 @@
             collective_id=0, has_side_effects=True, vmem_limit_bytes=VMEM_LIMIT
         ),
         name="shift",
-    )(drift, after, before, extra, r_tab, c_tab, hc)
+    )(offsets.transpose(scan_last), fractions.transpose(scan_last), after, before, r_tab, c_tab, hc)
 
     all_scan = lambda s, *_: (0, s, 0, 0)
     by_scan = lambda s, *_: (s, 0, 0)

time: 118 us -> 109 us (0.924)
  other arithmetic: 4.58 us -> 0.58 us
  local copies, waits for them, and re-layouts: 4.7 us -> 1.23 us
    unnamed x2 -> x0, other arithmetic: 2.68 us -> none
    slice x2 -> x0, local copies, waits for them, and re-layouts: 2.33 us -> none  [the longest x1 1.25 us: body(): after[:, :, length - LANES - 1:length - LANES]]
where the time goes in v5:
time: 109 us
  Pallas kernels  107 us (98%)
  local copies, waits for them, and re-layouts  1.23 us (1%)
    pallas_call x1, Pallas kernels, body(): pl.pallas_call(functools.partial(shift_kernel, n_row, n_col), out_shape=(...  44 us
    pallas_call x1, Pallas kernels, body(): pl.pallas_call(functools.partial(gather_kernel, n_row, n_col), out_shape=...  26.8 us
    pallas_call x1, Pallas kernels, body(): pl.pallas_call(functools.partial(band_kernel, n_row, n_col), out_shape=(s...  24.1 us
    pallas_call x1, Pallas kernels, body(): pl.pallas_call(functools.partial(total_kernel, n_row, n_col, float(n_row...  11.9 us

profile of v5, /device:TPU:0, one launch (start us, length us, event | category | flops | bytes accessed | tf_op | source)
XLA Modules:
  0.0 109.2 jit_solution(12551373553496627316)
XLA Ops:
  0.6 0.6 pad_add_fusion.place
  1.2 44.0 %shift.1 = (f32[4,256,1024]{2,1,0:T(8,128)}, f32[4,4,24,128]{3,2,1,0:T(8,128)}, f32[4,16,256]{2,1,0:T(8,128)}) custom-call(s32[2,1,1,4]{3,2,1,0:T(1,128)} %bitcast.8, s32[2,1,1,4]{3,2,1,0:T(1,128)} %bitcast.9, f32[4,256,1024]{2,1,0:T(8,128)} %after.1, f32[4,256,1024]{2,1,0:T(8,128)} %before_in.1, bf16[8,48,256]{2,1,0:T(8,128)(2,1)} %constant.25.clone.r_in, ...), custom_call_target="tpu_custom_call" | custom-call | tf_op jit(solution)/shard_map/shift/pallas_call | solution.py:622
  45.2 26.8 %gather.1 = (f32[2,4,8,1024]{3,2,1,0:T(8,128)}, f32[4,4,8,128]{3,2,1,0:T(8,128)}, f32[2,4,8,256]{3,2,1,0:T(8,128)}, f32[8,4,24,128]{3,2,1,0:T(8,128)}) custom-call(f32[4,256,1024]{2,1,0:T(8,128)} %get-tuple-element.13.diff, f32[4,4,24,128]{3,2,1,0:T(8,128)} %get-tuple-element.14.partial, f32[4,16,256]{2,1,0:T(8,128)} %get-tuple-element.15.edges), custom_call_target="tpu_custom_call" | custom-call | tf_op jit(solution)/shard_map/gather/pallas_call | solution.py:657
  72.0 24.1 %band.1 = (f32[4,256,1024]{2,1,0:T(8,128)}, f32[4,256,1024]{2,1,0:T(8,128)}, f32[4,2,8,128]{3,2,1,0:T(8,128)}) custom-call(s32[2]{0:T(128)} %pad_add_fusion.place, f32[4,256,1024]{2,1,0:T(8,128)} %get-tuple-element.13.diff, f32[2,4,8,1024]{3,2,1,0:T(8,128)} %get-tuple-element.16.rows_in, f32[4,4,8,128]{3,2,1,0:T(8,128)} %get-tuple-element.17.corners, ...), custom_call_target="tpu_custom_call" | custom-call | tf_op jit(solution)/shard_map/band/pallas_call | solution.py:678
  96.1 11.9 %total.1 = f32[2,4]{1,0:T(2,128)} custom-call(f32[4,2,8,128]{3,2,1,0:T(8,128)} %get-tuple-element.22.sums), custom_call_target="tpu_custom_call" | custom-call | tf_op jit(solution)/shard_map/total/pallas_call | solution.py:710
  108.0 1.2 %copy.18 = f32[2,4]{1,0:T(2,128)} copy(f32[2,4]{1,0:T(2,128)} %total.1) | data formatting | bytes 64
